TPU v7x, 32 devices: a whole 2x2x4 slice. The times are simulated.
32 devices in a mesh: groups: 2 (over y), seg: 4 (over z), slab: 2 (over x), comp: 2 (over core).
Axes of the slice: x: 2, y: 2, z: 4, core: 2. Of those that a mesh axis runs over, the one named last changes fastest.
Arguments:
- base: float32 [8, 3, 64, 4096], P(('groups', 'seg'), None, 'slab'), parts along dimension 0, may hold values from -6 to 6
- state: float32 [8, 2, 3, 64, 4096], P(('groups', 'seg'), 'comp', None, 'slab'), parts along dimension 0, may hold values from -6 to 6
- wavenumber: int32 [2], P('groups'), parts along dimension 0, may hold values from 1 to 4
- cutoff: int32 [6], P('groups'), parts along dimension 0, may hold values from 18 to 21, as said below
Outputs:
- base_gap: float32 [8, 3, 64, 4096], P(('groups', 'seg'), None, ('slab', 'comp')), parts along dimension 0
- state_gap: float32 [8, 2, 3, 64, 4096], P(('groups', 'seg'), 'comp', None, 'slab'), parts along dimension 0
There are 2 independent parts, one for each index of `groups`. A program takes and returns all parts, laid end to end along the dimension named above; each array names one. Nothing has to cross between parts.
Inputs may be any that keep to these rules, and one draw needn't show every extreme that they name: `cutoff`: each entry is at most one third of 64, rounded down, and at least that minus three; one entry always equals it.
All inputs are finite; a program needn't handle non-finite values.
Results may differ from a plain program's by a relative error of at most 0.0001.
Values sent between devices are 32-bit elements; how exact they have to be, the bound alone decides.
A program may use at most 128 MiB of HBM per device.

v0:
```python
import jax
import jax.numpy as jnp
from jax import lax
from jax.sharding import PartitionSpec as P

N = 64


viscosity = 0.025
time_step = 0.02
forcing_amp = 10.0
highest = lax.Precision.HIGHEST


def swapped(value, axis, apart):
    mask = 2**apart
    pairs = [(source, source ^ mask) for source in range(lax.axis_size(axis))]
    return lax.ppermute(value, axis, pairs)


def shifted(block, axis, distance):
    devices = range(lax.axis_size(axis))
    route = [((i - distance) % len(devices), i) for i in devices]
    return lax.ppermute(block, axis, route)


def wavenumbers(grid_points):
    position = jnp.arange(grid_points, dtype=jnp.int32)
    return jnp.where(position < grid_points // 2, position, position - grid_points)


def phases(first, second, grid_points):
    product = jnp.mod(first[:, None] * second[None, :], grid_points)
    return product.astype(jnp.float32) * (2.0 * jnp.pi / grid_points)


def combine(partial_value, columns):
    cosine_part = partial_value[0]
    sine_part = partial_value[1]
    real_part = cosine_part[..., :columns] - sine_part[..., columns:]
    imag_part = cosine_part[..., columns:] + sine_part[..., :columns]
    return jnp.concatenate([real_part, imag_part], axis=-1)


def times_unit(values, wave, columns):
    return jnp.concatenate([-wave * values[..., columns:], wave * values[..., :columns]], axis=-1)


def doubled(values):
    return jnp.concatenate([values, values], axis=-1)


def body(base, state, wavenumber, cutoff):
    grid_points = N
    base = base.reshape(base.shape[0], 3, base.shape[2], grid_points, grid_points)
    state = state.reshape(
        state.shape[0], state.shape[1], 3, state.shape[3], grid_points, grid_points
    )
    slab_rows = state.shape[3]
    half_rows = slab_rows // 2
    slab_count = lax.axis_size("slab")
    group_count = slab_count * lax.axis_size("comp")
    core_side = lax.axis_index("comp")
    block_number = lax.axis_index(("slab", "comp"))
    base_whole = base[0]
    base_half = lax.dynamic_slice_in_dim(base_whole, core_side * half_rows, half_rows, 1)
    own_state = state[0, 0]
    spectrum = wavenumbers(grid_points)
    one_third = grid_points // 3
    row_total = (2 * one_third + group_count) // group_count * group_count
    row_index = jnp.arange(row_total, dtype=jnp.int32)
    row_alive_mask = row_index <= 2 * one_third
    row_wave = jnp.where(row_index <= one_third, row_index, row_index - (2 * one_third + 1))
    row_wave = jnp.where(row_alive_mask, row_wave, 0)
    width = grid_points // 2
    rows_per_block = row_total // group_count
    alive_flags = row_alive_mask.astype(jnp.float32)
    grid_index = jnp.arange(grid_points, dtype=jnp.int32)
    column_index = grid_index[:width]
    angle_grid = phases(grid_index, grid_index, grid_points)
    angle_ahead = phases(grid_index, column_index, grid_points)
    angle_behind = phases(column_index, grid_index, grid_points)
    column_weight = jnp.where(column_index == 0, 1.0, 2.0).astype(jnp.float32)[:, None]
    forward_z = jnp.concatenate([jnp.cos(angle_ahead), -jnp.sin(angle_ahead)], axis=1)
    inverse_z = (
        jnp.concatenate(
            [jnp.cos(angle_behind) * column_weight, -jnp.sin(angle_behind) * column_weight], axis=0
        )
        / grid_points
    )
    phase_angle_rows = phases(row_wave, grid_index, grid_points)
    forward_transform_y = (
        jnp.stack([jnp.cos(phase_angle_rows), -jnp.sin(phase_angle_rows)])
        * alive_flags[None, :, None]
    )
    inverse_y = (
        jnp.stack([jnp.cos(phase_angle_rows).T, jnp.sin(phase_angle_rows).T])
        * alive_flags[None, None, :]
        / grid_points
    )
    forward_x = jnp.stack([jnp.cos(angle_grid), -jnp.sin(angle_grid)])
    inverse_x = jnp.stack([jnp.cos(angle_grid), jnp.sin(angle_grid)]) / grid_points
    table_ahead = forward_x.reshape(2, grid_points, slab_count, slab_rows)
    table_back = inverse_x.reshape(2, slab_count, slab_rows, grid_points)
    local_wave = lax.dynamic_slice_in_dim(row_wave, block_number * rows_per_block, rows_per_block)
    local_alive_mask = lax.dynamic_slice_in_dim(
        alive_flags, block_number * rows_per_block, rows_per_block
    )
    shape_local = (grid_points, rows_per_block, width)
    wave_x = jnp.broadcast_to(spectrum[:, None, None], shape_local)
    wave_y = jnp.broadcast_to(local_wave[None, :, None], shape_local)
    wave_z = jnp.broadcast_to(spectrum[:width][None, None, :], shape_local)
    inside = (
        (jnp.abs(wave_x) <= cutoff[0])
        & (jnp.abs(wave_y) <= cutoff[1])
        & (jnp.abs(wave_z) <= cutoff[2])
    )
    keep_mask = doubled(inside.astype(jnp.float32) * local_alive_mask[None, :, None])
    float_x = wave_x.astype(jnp.float32)
    float_y = wave_y.astype(jnp.float32)
    float_z = wave_z.astype(jnp.float32)
    ksquare = float_x * float_x + float_y * float_y + float_z * float_z
    safe_square = doubled(jnp.where(ksquare > 0, ksquare, jnp.ones_like(ksquare)))
    damping = doubled(1.0 / (1.0 + viscosity * time_step * ksquare))
    double_x = doubled(float_x)
    double_y = doubled(float_y)
    double_z = doubled(float_z)

    def project(field):
        divergence = (double_x * field[0] + double_y * field[1] + double_z * field[2]) / safe_square
        return jnp.stack(
            [
                field[0] - double_x * divergence,
                field[1] - double_y * divergence,
                field[2] - double_z * divergence,
            ]
        )

    def yz_forward(field):
        along_z = jnp.einsum("...z,zk->...k", field, forward_z, precision=highest)
        partial_value = jnp.einsum(
            "sry,...yk->s...rk", forward_transform_y, along_z, precision=highest
        )
        return combine(partial_value, width)

    def yz_inverse(modes):
        partial_value = jnp.einsum("syr,...rk->s...yk", inverse_y, modes, precision=highest)
        return jnp.einsum(
            "...k,kz->...z", combine(partial_value, width), inverse_z, precision=highest
        )

    def spectral(state_fields, base_fields):
        state_modes = yz_forward(state_fields)[:, :, None]
        base_modes = yz_forward(base_fields)[:, :, None]
        state_got = lax.all_to_all(
            state_modes, ("slab", "comp"), split_axis=4, concat_axis=2, tiled=True
        )
        base_got = lax.all_to_all(
            base_modes, ("slab", "comp"), split_axis=4, concat_axis=2, tiled=True
        )
        item_count = state_got.shape[0]
        part_count = state_got.shape[1]
        state_split = state_got.reshape(
            item_count, part_count, slab_count, 2, slab_rows, rows_per_block, 2 * width
        )
        state_partial = jnp.einsum(
            "srpx,ijpcxyk->sijcryk", table_ahead, state_split, precision=highest
        )
        base_lined = base_got.reshape(item_count, 1, grid_points, rows_per_block, 2 * width)
        base_partial = jnp.einsum("srx,ijxyk->sijryk", forward_x, base_lined, precision=highest)
        return (combine(state_partial, width), combine(base_partial, width))

    state_first, base_first = spectral(own_state[:, None], base_half[:, None])
    state_hat = state_first[:, 0] * keep_mask
    base_hat = base_first[:, 0] * keep_mask
    grad_hat = jnp.stack(
        [
            times_unit(base_hat, float_x, width),
            times_unit(base_hat, float_y, width),
            times_unit(base_hat, float_z, width),
        ],
        axis=1,
    )
    grad_hat = grad_hat.reshape(9, grid_points, rows_per_block, 2 * width)
    grad_partial = jnp.einsum("sxr,iryk->sixyk", inverse_x, grad_hat, precision=highest)
    grad_spread = combine(grad_partial, width).reshape(
        9, group_count, half_rows, rows_per_block, 2 * width
    )
    own_rows = yz_inverse(
        lax.all_to_all(grad_spread, ("slab", "comp"), split_axis=1, concat_axis=3, tiled=True)[:, 0]
    )
    other_rows = swapped(own_rows, "comp", 0)
    gradient = jnp.where(
        core_side == 0,
        jnp.concatenate([own_rows, other_rows], axis=1),
        jnp.concatenate([other_rows, own_rows], axis=1),
    )
    gradient = gradient.reshape(3, 3, slab_rows, grid_points, grid_points)
    gradient_half = lax.dynamic_slice_in_dim(gradient, core_side * half_rows, half_rows, 2)
    flux_terms = own_state[:, None] * base_whole[None, :]
    coupling_matrix = jnp.where(core_side == 0, gradient, jnp.swapaxes(gradient, 0, 1))
    coupling = jnp.sum(coupling_matrix * own_state[None, :], axis=1)
    forcing_phase = phases(wavenumber, grid_index, grid_points)[0]
    forcing = forcing_amp * jnp.sin(forcing_phase)[None, :, None]
    base_drive = jnp.sum(gradient_half * base_half[None, :], axis=1)
    base_drive = jnp.concatenate([base_drive[:1] - forcing[None], base_drive[1:]], axis=0)
    state_fields = jnp.concatenate([flux_terms, coupling[:, None]], axis=1)
    drive_modes, base_modes_two = spectral(state_fields, base_drive[:, None])
    orient = jnp.array([1.0, -1.0], dtype=jnp.float32)[None, :, None, None, None]
    divergence = (
        times_unit(drive_modes[:, 0], float_x, width)
        + times_unit(drive_modes[:, 1], float_y, width)
        + times_unit(drive_modes[:, 2], float_z, width)
    )
    state_drive = keep_mask * (orient * divergence + drive_modes[:, 3])
    new_hat = damping * project(state_hat - time_step * state_drive)
    base_new_hat = damping * project(base_hat - time_step * keep_mask * base_modes_two[:, 0])
    state_partial = jnp.einsum("spxr,icryk->sipcxyk", table_back, new_hat, precision=highest)
    state_back = combine(state_partial, width).reshape(
        3, group_count, slab_rows, rows_per_block, 2 * width
    )
    base_partial = jnp.einsum("sxr,iryk->sixyk", inverse_x, base_new_hat, precision=highest)
    base_back = combine(base_partial, width).reshape(
        3, group_count, half_rows, rows_per_block, 2 * width
    )
    state_got = lax.all_to_all(
        state_back, ("slab", "comp"), split_axis=1, concat_axis=3, tiled=True
    )
    base_got = lax.all_to_all(base_back, ("slab", "comp"), split_axis=1, concat_axis=3, tiled=True)
    state_new = yz_inverse(state_got[:, 0])
    base_new = yz_inverse(base_got[:, 0])
    base_later, later_state = shifted((base_half, own_state), "seg", -1)
    prior_state = shifted(own_state, "seg", 1)
    neighbour = jnp.where(core_side == 0, later_state, prior_state)
    base_gap = (base_new - base_later).reshape(1, 3, half_rows, grid_points * grid_points)
    state_gap = (state_new - neighbour).reshape(1, 1, 3, slab_rows, grid_points * grid_points)
    return (base_gap, state_gap)


def solution(mesh):
    return jax.shard_map(
        body,
        mesh=mesh,
        in_specs=(
            P(("groups", "seg"), None, "slab", None),
            P(("groups", "seg"), "comp", None, "slab", None),
            P("groups"),
            P("groups"),
        ),
        out_specs=(
            P(("groups", "seg"), None, ("slab", "comp"), None),
            P(("groups", "seg"), "comp", None, "slab", None),
        ),
        check_vma=False,
    )
```

profile of v0, /device:TPU:0, one launch (start us, length us, event | category | flops | bytes accessed | tf_op | source)
XLA Modules:
  0.0 482.5 jit_solution(9221279356138996617)
XLA Ops:
  10.7 4.4 all-to-all-start
  19.8 4.3 all-to-all-done
  34.8 7.3 %convolution_bitcast_fusion = f32[2,9,64,11,64]{2,4,0,3,1:T(8,128)S(1)} fusion(f32[9,64,11,64,1]{3,1,4,2,0:T(8,128)} %bitcast.400, f32[1,64,64]{2,1,0:T(8,128)S(1)} %get-tuple-element.106, f32[1,64,64]{2,1,0:T(8,128)S(1)} %copy-done.32), kind=kOutput, calls=%fused_computation.53 | convolution fusion | flops 622870528 | bytes 4898816 | tf_op jit(solution)/shard_map/sxr,iryk->sixyk/dot_general | solution.py:185
  52.4 4.4 all-to-all-start.1
  60.8 16.7 %all-to-all-done.1 = f32[4,1,101376]{2,1,0:T(1,128)} async-done(((f32[4,1,101376]{2,1,0:T(1,128)}), f32[4,1,101376]{2,1,0:T(1,128)}, u32[]{:S(2)}, u32[]{:S(2)}) %all-to-all-start.1) | async-done | bytes 1622048 | tf_op jit(solution)/shard_map/all_to_all | solution.py:190
  77.5 7.5 %reduce.1 = f32[4,101376]{1,0:T(4,128)} reduce(f32[4,1,101376]{2,1,0:T(1,128)} %all-to-all-done.1, f32[]{:T(128)} %broadcast.833), dimensions={1}, to_apply=%all_to_all.80.reduce_sub_computation | reduce | bytes 3244036 | tf_op jit(solution)/shard_map/all_to_all | solution.py:190
  85.0 4.3 reshape.640
  91.6 8.0 %fusion.22 = f32[2,9,16,64,64]{3,4,0,2,1:T(8,128)S(1)} fusion(f32[9,16,44,64,1]{3,1,2,0,4:T(8,128)S(1)} %bitcast.399, f32[1,64,44]{1,2,0:T(8,128)S(1)} %get-tuple-element.98, f32[1,64,44]{1,2,0:T(8,128)S(1)} %get-tuple-element.97, f32[44]{0:T(128)S(1)} %compare_convert_fusion), kind=kOutput, calls=%fused_computation.39 | convolution fusion | flops 622871040 | bytes 6363312 | tf_op jit(solution)/shard_map/syr,...rk->s...yk/dot_general | solution.py:147
  99.6 3.6 slice_bitcast_fusion.5
  103.2 3.6 slice_subtract_fusion.3
  106.8 9.4 %fusion.16 = f32[9,16,64,64]{3,2,1,0:T(8,128)} fusion(f32[9,16,64,32]{2,3,1,0:T(8,128)S(1)} %get-tuple-element.17, f32[9,16,64,32]{2,3,1,0:T(8,128)S(1)} %get-tuple-element.16, f32[32,64]{1,0:T(8,128)S(1)} %get-tuple-element.94, f32[32,64]{1,0:T(8,128)S(1)} %get-tuple-element.93), kind=kOutput, calls=%fused_computation.29 | convolution fusion | flops 453582848 | bytes 4734976 | tf_op jit(solution)/shard_map/...k,kz->...z/dot_general | solution.py:148
  116.3 9.1 %fusion.125 = f32[64,3,32,64]{3,0,2,1:T(8,128)S(1)} fusion(f32[3,32,64,64]{3,2,1,0:T(8,128)S(1)} %reshape.604, f32[64,64]{1,0:T(8,128)S(1)} %pad_maximum_fusion.21), kind=kOutput, calls=%fused_computation.263 | convolution fusion | flops 301989888 | bytes 3162112 | tf_op jit(solution)/shard_map/...z,zk->...k/dot_general | solution.py:140
  125.4 9.5 %fusion.32 = f32[2,3,1,32,44,64]{5,4,0,3,1,2:T(8,128)S(1)} fusion(f32[64,3,32,64]{3,0,2,1:T(8,128)S(1)} %fusion.125, f32[1,44,64]{2,1,0:T(8,128)S(1)} %get-tuple-element.103, f32[1,44,64]{2,1,0:T(8,128)S(1)} %get-tuple-element.102, f32[44]{0:T(128)S(1)} %compare_convert_fusion), kind=kOutput, calls=%fused_computation.63 | convolution fusion | flops 415247360 | bytes 3758256 | tf_op jit(solution)/shard_map/sry,...yk->s...rk/dot_general | solution.py:141
  143.0 9.2 %maximum_select_fusion = f32[3,3,32,64,64]{4,3,2,1,0:T(8,128)S(1)} fusion(f32[3,3,16,64,64]{4,3,2,1,0:T(8,128)} %bitcast.50, f32[3,3,16,64,64]{4,3,2,1,0:T(8,128)} %bitcast.49, pred[]{:T(512)S(6)} %eq.23), kind=kLoop, calls=%fused_computation.16 | loop fusion | flops 3538944 | bytes 9437185 | tf_op jit(solution)/shard_map/jit(_where)/select_n | solution.py:193
  154.3 9.4 %broadcast_multiply_fusion = (f32[3,3,32,64,64]{4,3,2,1,0:T(8,128)}, f32[3,32,64,64]{3,2,1,0:T(8,128)}) fusion(f32[3,32,64,64]{3,2,1,0:T(8,128)} %copy-done.2, f32[3,32,64,64]{3,2,1,0:T(8,128)} %copy-done, f32[3,3,32,64,64]{4,3,2,1,0:T(8,128)S(1)} %maximum_select_fusion, pred[]{:T(512)S(6)} %eq.23), kind=kLoop, calls=%fused_computation.33 | loop fusion | flops 4325376 | bytes 14155777 | tf_op jit(solution)/shard_map/mul | solution.py:200
  174.2 4.1 all-to-all-start.2
  178.4 13.1 %fusion = f32[3,4,32,64,64]{4,3,2,1,0:T(8,128)S(1)} fusion(f32[3,1,32,64,64]{4,3,2,1,0:T(8,128)S(1)} %bitcast.404, f32[3,3,32,64,64]{4,3,2,1,0:T(8,128)} %get-tuple-element.43, f32[64,64]{1,0:T(8,128)} %copy-done.19), kind=kOutput, calls=%fused_computation | convolution fusion | flops 1209532416 | bytes 12599296 | tf_op jit(solution)/shard_map/...z,zk->...k/dot_general | solution.py:140
  191.5 17.0 %fusion.10 = f32[2,3,4,32,44,64]{5,4,0,3,2,1:T(8,128)S(1)} fusion(f32[3,4,32,64,64]{4,3,2,1,0:T(8,128)S(1)} %fusion, f32[1,44,64]{2,1,0:T(8,128)S(1)} %copy-done.27, f32[1,44,64]{2,1,0:T(8,128)S(1)} %copy-done.24, f32[44]{0:T(128)S(1)} %compare_convert_fusion), kind=kOutput, calls=%fused_computation.25 | convolution fusion | flops 1660955648 | bytes 14964912 | tf_op jit(solution)/shard_map/sry,...yk->s...rk/dot_general | solution.py:141
  208.6 7.3 %slice_bitcast_fusion.1 = (f32[3,4,32,44,64]{4,3,2,1,0:T(8,128)}, f32[3,4,32,44,64]{4,3,2,1,0:T(8,128)}) fusion(f32[2,3,4,32,44,64]{5,4,0,3,2,1:T(8,128)S(1)} %fusion.10), kind=kLoop, calls=%fused_computation.15 | loop fusion | bytes 17301504 | tf_op jit(solution)/shard_map/squeeze | solution.py:38
  215.9 3.5 all-to-all-start.4
  235.1 4.3 all-to-all-start.3
  239.5 23.0 %slice_subtract_fusion = (f32[3,4,32,44,32]{4,3,2,1,0:T(8,128)}, f32[3,4,32,44,32]{4,3,2,1,0:T(8,128)}) fusion(f32[3,4,32,44,64]{4,3,2,1,0:T(8,128)} %get-tuple-element.11, f32[3,4,32,44,64]{4,3,2,1,0:T(8,128)} %get-tuple-element.10), kind=kLoop, calls=%fused_computation.13 | loop fusion | flops 1081344 | bytes 12976128 | tf_op jit(solution)/shard_map/sub | solution.py:40
  262.5 12.6 %maximum_bitcast_fusion = f32[3,4,1,32,44,64]{5,4,3,1,0,2:T(8,128)} fusion(f32[3,4,32,44,32]{4,3,2,1,0:T(8,128)} %get-tuple-element.9, f32[3,4,32,44,32]{4,3,2,1,0:T(8,128)} %get-tuple-element.8), kind=kLoop, calls=%fused_computation.17 | loop fusion | flops 1081344 | bytes 8650752 | tf_op jit(solution)/shard_map/broadcast_in_dim | solution.py:153
  275.0 9.9 %copy.208 = f32[3,4,1,32,44,64]{5,3,2,1,0,4:T(8,128)} copy(f32[3,4,1,32,44,64]{5,4,3,1,0,2:T(8,128)} %maximum_bitcast_fusion) | data formatting | bytes 8650752 | tf_op jit(solution)/shard_map/broadcast_in_dim | solution.py:153
  284.9 8.8 %reshape.645 = f32[4,1,270336]{2,1,0:T(1,128)} reshape(f32[44,3,4,1,32,64]{5,4,3,2,1,0:T(8,128)} %bitcast.397) | data formatting | bytes 8650752
  293.7 5.1 %all-to-all-start.5 = ((f32[4,1,270336]{2,1,0:T(1,128)}), f32[4,1,270336]{2,1,0:T(1,128)}, u32[]{:S(2)}, u32[]{:S(2)}) async-start(f32[4,1,270336]{2,1,0:T(1,128)} %reshape.645), calls=%async_computation.5 | async-start | bytes 8650752 | tf_op jit(solution)/shard_map/all_to_all | solution.py:155
  298.8 4.3 collective-permute-start.1
  309.0 5.7 %reduce.5 = f32[4,67584]{1,0:T(4,128)} reduce(f32[4,1,67584]{2,1,0:T(1,128)} %copy-done.11, f32[]{:T(128)} %broadcast.833), dimensions={1}, to_apply=%all_to_all.89.reduce_sub_computation | reduce | bytes 2162692 | tf_op jit(solution)/shard_map/all_to_all | solution.py:155
  314.6 3.6 reshape.648
  318.3 5.2 %convolution_bitcast_fusion.3 = f32[2,3,1,2,64,11,64]{4,6,0,5,3,1,2:T(8,128)S(1)} fusion(f32[3,2,2,32,11,64,1]{5,3,0,4,2,1,6:T(8,128)} %bitcast.405, f32[1,64,2,32]{1,3,2,0:T(8,128)} %get-tuple-element.92, f32[1,64,2,32]{1,3,2,0:T(8,128)S(1)} %get-tuple-element.91), kind=kOutput, calls=%fused_computation.65 | convolution fusion | flops 415244288 | bytes 3276800 | tf_op jit(solution)/shard_map/srpx,ijpcxyk->sijcryk/dot_general | solution.py:166
  325.9 3.9 reduce.3
  333.6 4.9 %convolution_bitcast_fusion.4 = f32[2,3,16,64,64]{3,4,0,2,1:T(8,128)} fusion(f32[3,16,44,64,1]{3,1,2,0,4:T(8,128)S(1)} %bitcast.410, f32[1,64,44]{1,2,0:T(8,128)S(1)} %copy-done.31, f32[1,64,44]{1,2,0:T(8,128)S(1)} %copy-done.29, f32[44]{0:T(128)S(1)} %copy-done.44), kind=kOutput, calls=%fused_computation.97 | convolution fusion | flops 207634944 | bytes 2136240 | tf_op jit(solution)/shard_map/syr,...rk->s...yk/dot_general | solution.py:147
  338.5 10.0 %all-to-all-done.5 = f32[4,1,270336]{2,1,0:T(1,128)} async-done(((f32[4,1,270336]{2,1,0:T(1,128)}), f32[4,1,270336]{2,1,0:T(1,128)}, u32[]{:S(2)}, u32[]{:S(2)}) %all-to-all-start.5) | async-done | bytes 4325408 | tf_op jit(solution)/shard_map/all_to_all | solution.py:155
  348.5 15.2 %reduce.4 = f32[4,270336]{1,0:T(4,128)} reduce(f32[4,1,270336]{2,1,0:T(1,128)} %all-to-all-done.5, f32[]{:T(128)} %broadcast.833), dimensions={1}, to_apply=%all_to_all.92.reduce_sub_computation | reduce | bytes 8650756 | tf_op jit(solution)/shard_map/all_to_all | solution.py:155
  363.6 9.6 %reshape.646 = f32[44,3,4,1,32,64]{5,4,3,2,1,0:T(8,128)} reshape(f32[4,270336]{1,0:T(4,128)} %reduce.4) | data formatting | bytes 8650752
  373.2 16.6 %fusion.13 = f32[2,3,4,2,64,11,64]{4,6,5,3,1,2,0:T(8,128)S(1)} fusion(f32[3,4,2,2,32,11,64,1]{6,4,1,0,5,3,2,7:T(8,128)} %bitcast.396, f32[1,64,2,32]{1,3,2,0:T(8,128)} %get-tuple-element.92, f32[1,64,2,32]{1,3,2,0:T(8,128)} %copy-done.36), kind=kOutput, calls=%fused_computation.26 | convolution fusion | flops 1660952576 | bytes 13008896 | tf_op jit(solution)/shard_map/srpx,ijpcxyk->sijcryk/dot_general | solution.py:166
  389.8 6.9 %slice_bitcast_fusion.3 = (f32[3,4,2,64,11,64]{3,5,4,2,0,1:T(8,128)}, f32[3,4,2,64,11,64]{3,5,4,2,0,1:T(8,128)}) fusion(f32[2,3,4,2,64,11,64]{4,6,5,3,1,2,0:T(8,128)S(1)} %fusion.13), kind=kLoop, calls=%fused_computation.22 | loop fusion | bytes 17301504 | tf_op jit(solution)/shard_map/squeeze | solution.py:38
  396.8 12.5 %slice_subtract_fusion.1 = (f32[3,4,2,64,11,32]{3,5,4,2,0,1:T(8,128)}, f32[3,4,2,64,11,32]{3,5,4,2,0,1:T(8,128)}) fusion(f32[3,4,2,64,11,64]{3,5,4,2,0,1:T(8,128)} %get-tuple-element.15, f32[3,4,2,64,11,64]{3,5,4,2,0,1:T(8,128)} %get-tuple-element.14), kind=kLoop, calls=%fused_computation.36 | loop fusion | flops 1081344 | bytes 12976128 | tf_op jit(solution)/shard_map/sub | solution.py:40
  409.3 3.6 fusion.36
  420.2 6.3 %convolution_bitcast_fusion.2 = f32[2,3,2,2,32,11,64]{6,4,2,0,5,3,1:T(8,128)S(1)} fusion(f32[1,2,64,11,64]{2,4,3,1,0:T(8,128)S(1)} %get-tuple-element.50, f32[1,2,64,11,64]{2,4,3,1,0:T(8,128)S(1)} %get-tuple-element.49, f32[1,2,64,11,64]{2,4,3,1,0:T(8,128)S(1)} %get-tuple-element.2, f32[64,11,64]{0,2,1:T(8,128)S(1)} %get-tuple-element.108, ...), kind=kOutput, calls=%fused_computation.64 | convolution fusion | flops 416063488 | bytes 3457024 | tf_op jit(solution)/shard_map/spxr,icryk->sipcxyk/dot_general | solution.py:218
  430.6 4.2 reshape.649
  434.8 4.5 all-to-all-start.6
  442.1 5.2 %fusion.66 = f32[3,16,64,64]{3,2,1,0:T(8,128)} fusion(f32[3,16,64,64]{3,2,1,0:T(8,128)} %collective-permute-done.1, f32[3,16,64,32]{2,3,1,0:T(8,128)S(1)} %get-tuple-element.46, f32[3,16,64,32]{2,3,1,0:T(8,128)S(1)} %get-tuple-element.45, f32[32,64]{1,0:T(8,128)S(1)} %copy-done.40, f32[32,64]{1,0:T(8,128)S(1)} %copy-done.38), kind=kOutput, calls=%fused_computation.119 | convolution fusion | flops 151396352 | bytes 2375680 | tf_op jit(solution)/shard_map/...k,kz->...z/dot_general | solution.py:148
  450.1 3.9 all-to-all-done.6
  453.9 5.6 %reduce.6 = f32[4,67584]{1,0:T(4,128)} reduce(f32[4,1,67584]{2,1,0:T(1,128)} %all-to-all-done.6, f32[]{:T(128)} %broadcast.833), dimensions={1}, to_apply=%all_to_all.95.reduce_sub_computation | reduce | bytes 2162692 | tf_op jit(solution)/shard_map/all_to_all | solution.py:226
  459.6 3.6 reshape.650
  464.9 6.4 %convolution_bitcast_fusion.1 = f32[2,3,32,64,64]{3,4,0,2,1:T(8,128)S(1)} fusion(f32[3,32,44,64,1]{3,1,2,0,4:T(8,128)S(1)} %bitcast.398, f32[1,64,44]{1,2,0:T(8,128)S(1)} %copy-done.31, f32[1,64,44]{1,2,0:T(8,128)S(1)} %copy-done.29, f32[44]{0:T(128)S(1)} %copy-done.45), kind=kOutput, calls=%fused_computation.54 | convolution fusion | flops 415252992 | bytes 4249776 | tf_op jit(solution)/shard_map/syr,...rk->s...yk/dot_general | solution.py:147
  473.5 6.7 %select_subtract_fusion = f32[3,32,64,64]{3,2,1,0:T(8,128)S(1)} fusion(f32[3,32,64,64]{3,2,1,0:T(8,128)} %collective-permute-done.2, f32[3,32,64,64]{3,2,1,0:T(8,128)} %collective-permute-done.3, pred[]{:T(512)S(6)} %eq.23, f32[32,64]{1,0:T(8,128)S(1)} %copy-done.40, f32[32,64]{1,0:T(8,128)S(1)} %copy-done.38, f32[3,32,64,32]{2,3,1,0:T(8,128)S(1)} %get-tuple-element.28, ...), kind=kOutput, calls=%fused_computation.52 | convolution fusion | flops 303177728 | bytes 6307841 | tf_op jit(solution)/shard_map/...k,kz->...z/dot_general | solution.py:148
  (280 shorter events, 111.5 us)
Async XLA Ops:
  0.6 16.8 %copy-start.52 = (s32[44]{0:T(128)}, s32[44]{0:T(128)S(1)}, u32[]{:S(2)}) copy-start(s32[44]{0:T(128)S(1)} %compare_select_fusion.7) | copy-start | bytes 532
  0.7 190.9 %copy-start.43 = (f32[44]{0:T(128)}, f32[44]{0:T(128)S(1)}, u32[]{:S(2)}) copy-start(f32[44]{0:T(128)S(1)} %compare_convert_fusion) | copy-start | bytes 532
  3.5 121.9 %copy-start.22 = (f32[1,44,64]{2,1,0:T(8,128)}, f32[1,44,64]{2,1,0:T(8,128)S(1)}, u32[]{:S(2)}) copy-start(f32[1,44,64]{2,1,0:T(8,128)S(1)} %get-tuple-element.102) | copy-start | bytes 33796
  3.5 121.9 %copy-start.25 = (f32[1,44,64]{2,1,0:T(8,128)}, f32[1,44,64]{2,1,0:T(8,128)S(1)}, u32[]{:S(2)}) copy-start(f32[1,44,64]{2,1,0:T(8,128)S(1)} %get-tuple-element.103) | copy-start | bytes 33796
  3.8 112.5 %copy-start.19 = (f32[64,64]{1,0:T(8,128)}, f32[64,64]{1,0:T(8,128)S(1)}, u32[]{:S(2)}) copy-start(f32[64,64]{1,0:T(8,128)S(1)} %pad_maximum_fusion.21) | copy-start | bytes 49156
  8.8 7.4 %copy-start.56 = (s32[3]{0:T(128)S(1)}, s32[3]{0:T(128)}, u32[]{:S(2)}) copy-start(s32[3]{0:T(128)} %param.8) | copy-start | bytes 40
  10.7 13.4 %all-to-all-start = ((f32[4,1,33792]{2,1,0:T(1,128)}), f32[4,1,33792]{2,1,0:T(1,128)S(1)}, u32[]{:S(2)}, u32[]{:S(2)}) async-start(f32[4,1,33792]{2,1,0:T(1,128)} %reshape.637), calls=%async_computation | async-start | bytes 1081344 | tf_op jit(solution)/shard_map/all_to_all | solution.py:158
  15.1 291.2 %copy-start.48 = (f32[64]{0:T(128)}, f32[64]{0:T(128)S(1)}, u32[]{:S(2)}) copy-start(f32[64]{0:T(128)S(1)} %fusion.194) | copy-start | bytes 772
  15.3 12.2 %copy-start.34 = (f32[1,64,64]{2,1,0:T(8,128)}, f32[1,64,64]{2,1,0:T(8,128)S(1)}, u32[]{:S(2)}) copy-start(f32[1,64,64]{2,1,0:T(8,128)S(1)} %get-tuple-element.107) | copy-start | bytes 49156
  15.3 14.8 %copy-start.57 = (f32[64]{0:T(128)}, f32[64]{0:T(128)S(1)}, u32[]{:S(2)}) copy-start(f32[64]{0:T(128)S(1)} %fusion.195) | copy-start | bytes 772
  15.5 14.6 %copy-start.54 = (f32[11]{0:T(128)}, f32[11]{0:T(128)S(1)}, u32[]{:S(2)}) copy-start(f32[11]{0:T(128)S(1)} %get-tuple-element.6) | copy-start | bytes 136
  15.5 290.8 %copy-start.46 = (f32[11]{0:T(128)}, f32[11]{0:T(128)S(1)}, u32[]{:S(2)}) copy-start(f32[11]{0:T(128)S(1)} %get-tuple-element.7) | copy-start | bytes 136
  19.7 10.2 %copy-start.14 = (f32[64,11,64]{0,2,1:T(8,128)}, f32[64,11,64]{0,2,1:T(8,128)S(1)}, u32[]{:S(2)}) copy-start(f32[64,11,64]{0,2,1:T(8,128)S(1)} %get-tuple-element.86) | copy-start | bytes 540676
  19.7 285.6 %copy-start.50 = (f32[32]{0:T(128)}, f32[32]{0:T(128)S(1)}, u32[]{:S(2)}) copy-start(f32[32]{0:T(128)S(1)} %slice_convert_fusion) | copy-start | bytes 388
  19.7 10.3 %copy-start.59 = (f32[32]{0:T(128)}, f32[32]{0:T(128)S(1)}, u32[]{:S(2)}) copy-start(f32[32]{0:T(128)S(1)} %get-tuple-element.96) | copy-start | bytes 388
  19.8 120.8 %copy-start.63 = (f32[32]{0:T(128)}, f32[32]{0:T(128)S(1)}, u32[]{:S(2)}) copy-start(f32[32]{0:T(128)S(1)} %get-tuple-element.95) | copy-start | bytes 388
  52.4 25.1 %all-to-all-start.1 = ((f32[4,1,101376]{2,1,0:T(1,128)}), f32[4,1,101376]{2,1,0:T(1,128)}, u32[]{:S(2)}, u32[]{:S(2)}) async-start(f32[4,1,101376]{2,1,0:T(1,128)} %reshape.639), calls=%async_computation.1 | async-start | bytes 3244032 | tf_op jit(solution)/shard_map/all_to_all | solution.py:190
  56.9 83.7 %copy-start.64 = (f32[11]{0:T(128)}, f32[11]{0:T(128)S(1)}, u32[]{:S(2)}) copy-start(f32[11]{0:T(128)S(1)} %mul.711) | copy-start | bytes 136
  60.4 55.8 %copy-start = (f32[3,32,64,64]{3,2,1,0:T(8,128)}, f32[3,32,64,64]{3,2,1,0:T(8,128)S(1)}, u32[]{:S(2)}) copy-start(f32[3,32,64,64]{3,2,1,0:T(8,128)S(1)} %reshape.604) | copy-start | bytes 4718596
  60.6 46.2 %copy-start.37 = (f32[32,64]{1,0:T(8,128)}, f32[32,64]{1,0:T(8,128)S(1)}, u32[]{:S(2)}) copy-start(f32[32,64]{1,0:T(8,128)S(1)} %get-tuple-element.93) | copy-start | bytes 24580
  60.6 46.2 %copy-start.39 = (f32[32,64]{1,0:T(8,128)}, f32[32,64]{1,0:T(8,128)S(1)}, u32[]{:S(2)}) copy-start(f32[32,64]{1,0:T(8,128)S(1)} %get-tuple-element.94) | copy-start | bytes 24580
  60.8 30.8 %copy-start.28 = (f32[1,64,44]{1,2,0:T(8,128)}, f32[1,64,44]{1,2,0:T(8,128)S(1)}, u32[]{:S(2)}) copy-start(f32[1,64,44]{1,2,0:T(8,128)S(1)} %get-tuple-element.97) | copy-start | bytes 33796
  60.8 30.8 %copy-start.30 = (f32[1,64,44]{1,2,0:T(8,128)}, f32[1,64,44]{1,2,0:T(8,128)S(1)}, u32[]{:S(2)}) copy-start(f32[1,64,44]{1,2,0:T(8,128)S(1)} %get-tuple-element.98) | copy-start | bytes 33796
  116.2 26.8 %collective-permute-start = (f32[9,16,64,64]{3,2,1,0:T(8,128)}, f32[9,16,64,64]{3,2,1,0:T(8,128)}, u32[]{:S(2)}, u32[]{:S(2)}) collective-permute-start(f32[9,16,64,64]{3,2,1,0:T(8,128)} %fusion.16), channel_id=1, source_target_pairs={{0,1},{1,0},{2,3},{3,2},{4,5},{5,4},{6,7},{7,6},{8,9},{9,8},{10,11... | collective-permute-start | bytes 7077896 | tf_op jit(solution)/shard_map/ppermute | solution.py:18
  143.0 9.2 %copy-start.4 = (f32[3,16,64,64]{3,2,1,0:T(8,128)S(1)}, f32[3,16,64,64]{3,2,1,0:T(8,128)}, u32[]{:S(2)}) copy-start(f32[3,16,64,64]{3,2,1,0:T(8,128)} %copy-done.3) | copy-start | bytes 2359300
  170.2 8.2 %copy-start.5 = (f32[3,32,64,64]{3,2,1,0:T(8,128)S(1)}, f32[3,32,64,64]{3,2,1,0:T(8,128)}, u32[]{:S(2)}) copy-start(f32[3,32,64,64]{3,2,1,0:T(8,128)} %get-tuple-element.44) | copy-start | bytes 4718596
  174.2 41.7 %all-to-all-start.2 = ((f32[4,1,33792]{2,1,0:T(1,128)}), f32[4,1,33792]{2,1,0:T(1,128)}, u32[]{:S(2)}, u32[]{:S(2)}) async-start(f32[4,1,33792]{2,1,0:T(1,128)} %reshape.641), calls=%async_computation.2 | async-start | bytes 1081344 | tf_op jit(solution)/shard_map/all_to_all | solution.py:158
  178.4 13.1 %copy-start.24 = (f32[1,44,64]{2,1,0:T(8,128)S(1)}, f32[1,44,64]{2,1,0:T(8,128)}, u32[]{:S(2)}) copy-start(f32[1,44,64]{2,1,0:T(8,128)} %copy-done.22) | copy-start | bytes 33796
  178.4 13.1 %copy-start.27 = (f32[1,44,64]{2,1,0:T(8,128)S(1)}, f32[1,44,64]{2,1,0:T(8,128)}, u32[]{:S(2)}) copy-start(f32[1,44,64]{2,1,0:T(8,128)} %copy-done.25) | copy-start | bytes 33796
  215.9 19.2 %all-to-all-start.4 = ((f32[4,1,67584]{2,1,0:T(1,128)}), f32[4,1,67584]{2,1,0:T(1,128)S(1)}, u32[]{:S(2)}, u32[]{:S(2)}) async-start(f32[4,1,67584]{2,1,0:T(1,128)} %reshape.647), calls=%async_computation.4 | async-start | bytes 2162688 | tf_op jit(solution)/shard_map/all_to_all | solution.py:155
  235.1 27.3 %copy-start.11 = (f32[4,1,67584]{2,1,0:T(1,128)}, f32[4,1,67584]{2,1,0:T(1,128)S(1)}, u32[]{:S(2)}) copy-start(f32[4,1,67584]{2,1,0:T(1,128)S(1)} %all-to-all-done.4) | copy-start | bytes 3244036
  235.1 58.5 %all-to-all-start.3 = ((f32[4,1,33792]{2,1,0:T(1,128)}), f32[4,1,33792]{2,1,0:T(1,128)}, u32[]{:S(2)}, u32[]{:S(2)}) async-start(f32[4,1,33792]{2,1,0:T(1,128)} %reshape.643), calls=%async_computation.3 | async-start | bytes 1081344 | tf_op jit(solution)/shard_map/all_to_all | solution.py:229
  293.7 9.5 %copy-start.1 = (f32[3,32,64,64]{3,2,1,0:T(8,128)S(1)}, f32[3,32,64,64]{3,2,1,0:T(8,128)}, u32[]{:S(2)}) copy-start(f32[3,32,64,64]{3,2,1,0:T(8,128)} %copy-done) | copy-start | bytes 4718596
  293.7 54.8 %all-to-all-start.5 = ((f32[4,1,270336]{2,1,0:T(1,128)}), f32[4,1,270336]{2,1,0:T(1,128)}, u32[]{:S(2)}, u32[]{:S(2)}) async-start(f32[4,1,270336]{2,1,0:T(1,128)} %reshape.645), calls=%async_computation.5 | async-start | bytes 8650752 | tf_op jit(solution)/shard_map/all_to_all | solution.py:155
  298.8 142.9 %collective-permute-start.1 = (f32[3,16,64,64]{3,2,1,0:T(8,128)}, f32[3,16,64,64]{3,2,1,0:T(8,128)}, u32[]{:S(2)}, u32[]{:S(2)}) collective-permute-start(f32[3,16,64,64]{3,2,1,0:T(8,128)} %copy-done.3), channel_id=1, source_target_pairs={{4,0},{8,4},{12,8},{0,12},{5,1},{9,5},{13,9},{1,13},{6,2},{10,6},{... | collective-permute-start | bytes 2359304 | tf_op jit(solution)/shard_map/ppermute | solution.py:24
  303.2 170.1 %collective-permute-start.2 = (f32[3,32,64,64]{3,2,1,0:T(8,128)S(1)}, f32[3,32,64,64]{3,2,1,0:T(8,128)}, u32[]{:S(2)}, u32[]{:S(2)}) collective-permute-start(f32[3,32,64,64]{3,2,1,0:T(8,128)S(1)} %copy-done.1), channel_id=1, source_target_pairs={{4,0},{8,4},{12,8},{0,12},{5,1},{9,5},{13,9},{1,13},{6,2},{10,6},{... | collective-permute-start | bytes 4718600 | tf_op jit(solution)/shard_map/ppermute | solution.py:24
  303.6 169.9 %collective-permute-start.3 = (f32[3,32,64,64]{3,2,1,0:T(8,128)S(1)}, f32[3,32,64,64]{3,2,1,0:T(8,128)}, u32[]{:S(2)}, u32[]{:S(2)}) collective-permute-start(f32[3,32,64,64]{3,2,1,0:T(8,128)S(1)} %copy-done.1), channel_id=1, source_target_pairs={{12,0},{0,4},{4,8},{8,12},{13,1},{1,5},{5,9},{9,13},{14,2},{2,6},{... | collective-permute-start | bytes 4718600 | tf_op jit(solution)/shard_map/ppermute | solution.py:24
  308.1 10.1 %copy-start.36 = (f32[1,64,2,32]{1,3,2,0:T(8,128)}, f32[1,64,2,32]{1,3,2,0:T(8,128)S(1)}, u32[]{:S(2)}) copy-start(f32[1,64,2,32]{1,3,2,0:T(8,128)S(1)} %get-tuple-element.91) | copy-start | bytes 49156
  329.8 3.8 copy-start.29
  329.8 3.9 copy-start.31
  409.3 3.7 copy-start.49
  409.3 3.7 copy-start.58
  409.3 4.0 copy-start.47
  409.3 4.0 copy-start.55
  413.0 3.5 slice-start.2
  414.2 3.1 copy-start.15
  414.2 3.1 copy-start.65
  434.8 19.1 %all-to-all-start.6 = ((f32[4,1,67584]{2,1,0:T(1,128)}), f32[4,1,67584]{2,1,0:T(1,128)}, u32[]{:S(2)}, u32[]{:S(2)}) async-start(f32[4,1,67584]{2,1,0:T(1,128)} %reshape.649), calls=%async_computation.6 | async-start | bytes 2162688 | tf_op jit(solution)/shard_map/all_to_all | solution.py:226
  (34 other events, 58.7 us)
where the time goes:
time: 490 us; the launch traced here: 483 us
  other arithmetic  145 us (30%)
  matrix products  137 us (28%)
  local copies, waits for them, and re-layouts  124 us (25%)
  starting transfers between devices  37 us (8%)
  waiting for transfers between devices  35 us (7%)
    unnamed x154, local copies, waits for them, and re-layouts  57.1 us
    sub x14, other arithmetic, combine(): real_part = cosine_part[..., :columns] - sine_part[..., columns:]  47.3 us
    dot_general x4, matrix products, yz_forward(): jnp.einsum('sry,...yk->s...rk', forward_transform_y, along_z, precision=h...  30.7 us
    squeeze x14, local copies, waits for them, and re-layouts, combine(): cosine_part = partial_value[0]  25 us
    dot_general x4, matrix products, yz_forward(): along_z = jnp.einsum('...z,zk->...k', field, forward_z, precision=highest)  25 us
    dot_general x2, matrix products, spectral(): jnp.einsum('srpx,ijpcxyk->sijcryk', table_ahead, state_split, precision=h...  21.8 us
    dot_general x3, matrix products, yz_inverse(): jnp.einsum('...k,kz->...z', combine(partial_value, width), inverse_z, pre...  21.2 us
    all_to_all x2, other arithmetic, spectral(): lax.all_to_all(state_modes, ('slab', 'comp'), split_axis=4, concat_axis=2...  20.8 us
  transfers between devices with their start and end apart: 11, of which 5 were waited for; matrix products, arithmetic and copies ran while one was open for 59% of the time, Pallas kernels for 0%

commit v1 on v0

v1 whole, which is shorter than its diff:
```python
import functools

import jax
import jax.numpy as jnp
import ml_dtypes
import numpy as np
from jax import lax
from jax.experimental import pallas as pl
from jax.experimental.pallas import tpu as pltpu
from jax.sharding import PartitionSpec as P

N = 64
THIRD = N // 3
LOW = THIRD - 3
KZ = THIRD + 1
KP = 24
MP = 48
PAIRS = N // 2
viscosity = 0.025
time_step = 0.02
forcing_amp = 10.0
f32 = jnp.float32
bf16 = jnp.bfloat16

NN = (((1,), (0,)), ((), ()))
NT = (((1,), (1,)), ((), ()))
TN = (((0,), (0,)), ((), ()))


def split(value):
    high = value.astype(bf16)
    return high, (value - high.astype(f32)).astype(bf16)


def dot3(left, right, dims):
    dot = functools.partial(lax.dot_general, dimension_numbers=dims, preferred_element_type=f32)
    return dot(left[0], right[0]) + (dot(left[0], right[1]) + dot(left[1], right[0]))


def table(values):
    values = np.asarray(values, np.float32)
    high = values.astype(ml_dtypes.bfloat16)
    low = (values - high.astype(np.float32)).astype(ml_dtypes.bfloat16)
    return np.stack([high, low], axis=-3)


def signed():
    m = np.arange(2 * THIRD + 1)
    return np.where(m <= THIRD, m, m - (2 * THIRD + 1))


def angles(first, second):
    return np.mod(np.outer(first, second), N) * (2 * np.pi / N)


def cuts():
    return range(LOW, THIRD + 1)


def z_tables():
    plain, ik = [], []
    k = np.arange(KZ)
    a = angles(k, np.arange(N))
    for cut in cuts():
        keep = 1.0 * (k <= cut)[:, None]
        w = np.zeros((2, KP, N))
        v = np.zeros((2, KP, N))
        w[0, :KZ], w[1, :KZ] = keep * np.cos(a), -keep * np.sin(a)
        v[0, :KZ], v[1, :KZ] = keep * k[:, None] * np.sin(a), keep * k[:, None] * np.cos(a)
        plain.append(np.kron(np.eye(2), w.reshape(2 * KP, N)))
        ik.append(np.kron(np.eye(2), v.reshape(2 * KP, N)))
    return table(np.stack([np.stack(plain), np.stack(ik)], axis=1))


def y_tables():
    out = []
    m = signed()
    count = len(m)
    a = angles(m, np.arange(N))
    for cut in cuts():
        keep = 1.0 * (np.abs(m) <= cut)[:, None]
        c, s = keep * np.cos(a), keep * np.sin(a)
        w = np.zeros((2, MP, N, 2))
        w[0, :count, :, 0], w[0, :count, :, 1] = c, s
        w[1, :count, :, 0], w[1, :count, :, 1] = -s, c
        v = np.zeros_like(w)
        v[0, :count] = -m[:, None, None] * w[1, :count]
        v[1, :count] = m[:, None, None] * w[0, :count]
        out.append(np.stack([w.reshape(2 * MP, 2 * N), v.reshape(2 * MP, 2 * N)]))
    return table(np.stack(out))


def y_back():
    m = signed()
    count = len(m)
    a = angles(np.arange(N), m)
    c, s = np.cos(a) / N, np.sin(a) / N
    w = np.zeros((N, 2, 2, MP))
    w[:, 0, 0, :count], w[:, 0, 1, :count] = c, -s
    w[:, 1, 0, :count], w[:, 1, 1, :count] = s, c
    v = np.zeros_like(w)
    v[:, :, 0, :count] = m * w[:, :, 1, :count]
    v[:, :, 1, :count] = -m * w[:, :, 0, :count]
    return table(np.stack([w.reshape(2 * N, 2 * MP), v.reshape(2 * N, 2 * MP)]))


def z_back():
    k = np.arange(KZ)
    a = angles(k, np.arange(N))
    weight = (np.where(k == 0, 1.0, 2.0) / N)[:, None]
    w = np.zeros((2, KP, N))
    w[0, :KZ], w[1, :KZ] = weight * np.cos(a), -weight * np.sin(a)
    v = np.zeros_like(w)
    v[0, :KZ] = k[:, None] * w[1, :KZ]
    v[1, :KZ] = -k[:, None] * w[0, :KZ]
    pair = lambda t: np.kron(np.eye(2), t.reshape(2 * KP, N))
    return table(np.stack([pair(w), pair(v)]))


def x_filters(slabs):
    rows = N // slabs
    out = []
    x = np.arange(N)
    for cut in cuts():
        n = np.arange(-cut, cut + 1)
        d = np.mod(x[:, None] - x[None, :], N)
        phase = 2 * np.pi / N * n[:, None, None] * -d
        plain = np.cos(phase).sum(0) / N
        deriv = (-n[:, None, None] * np.sin(phase)).sum(0) / N
        both = np.stack([plain, deriv]).reshape(2, slabs, rows, slabs, rows)
        wide = np.zeros((slabs, 2, slabs, 3, rows, 3, rows))
        for i in range(3):
            wide[:, :, :, i, :, i, :] = both.transpose(3, 0, 1, 2, 4)
        out.append(wide.reshape(slabs, 2, slabs, 3 * rows, 3 * rows))
    return table(np.stack(out))


def x_tables(slabs):
    rows = N // slabs
    n = signed()
    count = len(n)
    a = angles(np.arange(N), n).reshape(slabs, rows, count)
    out = []
    for cut in cuts():
        keep = 1.0 * (np.abs(n) <= cut)
        c, s = np.cos(a) * keep, np.sin(a) * keep
        w = np.zeros((slabs, 2, 2, 3, rows, 3, 2, 64))
        for i in range(3):
            w[:, 0, 0, i, :, i, 0, :count] = c
            w[:, 0, 0, i, :, i, 1, :count] = -s
            w[:, 0, 1, i, :, i, 0, :count] = s
            w[:, 0, 1, i, :, i, 1, :count] = c
        w[:, 1, :, :, :, :, 0, :count] = -n * w[:, 0, :, :, :, :, 1, :count]
        w[:, 1, :, :, :, :, 1, :count] = n * w[:, 0, :, :, :, :, 0, :count]
        out.append(w.reshape(slabs, 2, 2, 3 * rows, 384))
    return table(np.stack(out))


def x_back(slabs):
    rows = N // slabs
    n = signed()
    count = len(n)
    a = angles(n, np.arange(N)).reshape(count, slabs, rows).transpose(1, 0, 2)
    c, s = np.cos(a) / N, np.sin(a) / N
    w = np.zeros((slabs, 2, 3, 2, 64, 3, rows))
    for i in range(3):
        w[:, 0, i, 0, :count, i] = c
        w[:, 0, i, 1, :count, i] = -s
        w[:, 1, i, 0, :count, i] = s
        w[:, 1, i, 1, :count, i] = c
    return table(w.reshape(slabs, 2, 384, 3 * rows))


def both(ref, *index):
    return ref[(*index, 0)], ref[(*index, 1)]


def lanes(p):
    return pl.ds(pl.multiple_of(p * 128, 128), 128)


def pair_rows(p):
    return pl.ds(pl.multiple_of(p * 4 * KP, 8), 4 * KP)


def column(k):
    return pl.ds(k, 2 * N, stride=KP)


def flat(block):
    return block.reshape(block.shape[0] * block.shape[1], block.shape[2])


def loop(count, unroll, step):
    def go(i, carry):
        step(i)
        return carry

    lax.fori_loop(0, count, go, 0, unroll=unroll)


def base_ahead(base_ref, wz_ref, wy_ref, out_ref, work):
    def along_z(p):
        block = split(flat(base_ref[:, :, lanes(p)]))
        work[pair_rows(p), :] = dot3(both(wz_ref, 0), block, NT)

    loop(PAIRS, 4, along_z)

    def along_y(k):
        out_ref[k] = dot3(both(wy_ref, 0), split(work[column(k), :]), NN)

    loop(KZ, 2, along_y)


def flux_ahead(base_ref, state_ref, wz_ref, wy_ref, g_ref, f_ref, work_a, work_b, work_f):
    scale = jnp.where(lax.axis_index("comp") == 0, -time_step, time_step).astype(f32)

    def along_z(p):
        state = state_ref[:, :, lanes(p)]
        base = base_ref[:, :, lanes(p)]
        scaled = state * scale
        f0, f1, f2 = (split(flat(scaled * base[j][None])) for j in range(3))
        plain = both(wz_ref, 0)
        work_a[pair_rows(p), :] = dot3(plain, split(flat(state)), NT) + dot3(
            both(wz_ref, 1), f2, NT
        )
        work_b[pair_rows(p), :] = dot3(plain, f1, NT)
        work_f[pair_rows(p), :] = dot3(plain, f0, NT)

    loop(PAIRS, 2, along_z)

    def along_y(k):
        plain = both(wy_ref, 0)
        g_ref[k] = dot3(plain, split(work_a[column(k), :]), NN) + dot3(
            both(wy_ref, 1), split(work_b[column(k), :]), NN
        )
        f_ref[k] = dot3(plain, split(work_f[column(k), :]), NN)

    loop(KZ, 2, along_y)


def gradients(
    slabs, got_ref, base_ref, state_ref, force_ref, pd_ref, yb_ref, zb_ref, wz_ref, wy_ref,
    xt_ref, g_ref, f_ref, out_ref, base_out_ref, work_0, work_1, work_2,
):
    tangent = lax.axis_index("comp") == 0

    def back_y(k):
        sources = [split(got_ref[s, k]) for s in range(slabs)]

        def across(kind):
            total = dot3(sources[0], both(pd_ref, kind, 0), NN)
            for s in range(1, slabs):
                total = total + dot3(sources[s], both(pd_ref, kind, s), NN)
            return split(total)

        plain, deriv = across(0), across(1)
        work_0[column(k), :] = dot3(both(yb_ref, 0), deriv, NN)
        work_1[column(k), :] = dot3(both(yb_ref, 1), plain, NN)
        work_2[column(k), :] = dot3(both(yb_ref, 0), plain, NN)

    def clear(p):
        zero = jnp.zeros((4 * KP, work_0.shape[1]), f32)
        work_0[pair_rows(p), :] = zero
        work_1[pair_rows(p), :] = zero
        work_2[pair_rows(p), :] = zero

    loop(PAIRS, 2, clear)
    loop(KZ, 2, back_y)

    def grid_space(p):
        state = state_ref[:, :, lanes(p)]
        base = base_ref[:, :, lanes(p)]
        grad = []
        for work, kind in ((work_0, 0), (work_1, 0), (work_2, 1)):
            rows = dot3(split(work[pair_rows(p), :]), both(zb_ref, kind), TN)
            grad.append(rows.reshape(base.shape))
        coupled, driven = [], []
        for i in range(3):
            total = 0.0
            drive = 0.0
            for j in range(3):
                total = total + jnp.where(tangent, grad[j][i], grad[i][j]) * state[j]
                drive = drive + grad[j][i] * base[j]
            if i == 0:
                drive = drive - force_ref[:, lanes(p)]
            coupled.append(-time_step * total)
            driven.append(base[i] - time_step * drive)
        plain = both(wz_ref, 0)
        work_0[pair_rows(p), :] = dot3(plain, split(jnp.concatenate(coupled, axis=0)), NT)
        work_1[pair_rows(p), :] = dot3(plain, split(jnp.concatenate(driven, axis=0)), NT)

    loop(PAIRS, 2, grid_space)

    def ahead_x(k):
        plain = both(wy_ref, 0)
        total = g_ref[k] + dot3(plain, split(work_0[column(k), :]), NN)
        driven = dot3(plain, split(work_1[column(k), :]), NN)
        outer = f_ref[k]
        state_modes, base_modes = 0.0, 0.0
        for d in range(2):
            rows = slice(d * MP, (d + 1) * MP)
            state_modes = state_modes + dot3(split(total[rows]), both(xt_ref, 0, d), NN)
            state_modes = state_modes + dot3(split(outer[rows]), both(xt_ref, 1, d), NN)
            base_modes = base_modes + dot3(split(driven[rows]), both(xt_ref, 0, d), NN)
        out_ref[k] = state_modes
        base_out_ref[k] = base_modes

    loop(KZ, 2, ahead_x)


def finish(count, *refs):
    parts, (near_ref, xb_ref, yb_ref, zb_ref, out_ref, work) = refs[:count], refs[count:]
    column_n = lax.rem(lax.broadcasted_iota(jnp.int32, (MP, 128), 1), 64)
    row_m = lax.broadcasted_iota(jnp.int32, (MP, 128), 0)
    wrap = lambda v: jnp.where(v <= THIRD, v, v - (2 * THIRD + 1)).astype(f32)
    wave_x, wave_y = wrap(column_n), wrap(row_m)
    flat_square = wave_x * wave_x + wave_y * wave_y

    def clear(p):
        work[pair_rows(p), :] = jnp.zeros((4 * KP, work.shape[1]), f32)

    loop(PAIRS, 2, clear)

    def spectral(k):
        modes = parts[0][k]
        for part in parts[1:]:
            modes = modes + part[k]
        wave_z = jnp.asarray(k, jnp.int32).astype(f32)
        square = flat_square + wave_z * wave_z
        safe = jnp.where(square > 0, square, 1.0)
        damping = 1.0 / (1.0 + viscosity * time_step * square)
        w = [modes[:, i * 128 : (i + 1) * 128] for i in range(3)]
        divergence = (wave_x * w[0] + wave_y * w[1] + wave_z * w[2]) / safe
        new = [
            damping * (w[0] - wave_x * divergence),
            damping * (w[1] - wave_y * divergence),
            damping * (w[2] - wave_z * divergence),
        ]
        new = split(jnp.concatenate(new, axis=1))
        rows = [dot3(new, both(xb_ref, d), NN) for d in range(2)]
        work[column(k), :] = dot3(both(yb_ref, 0), split(jnp.concatenate(rows, axis=0)), NN)

    loop(KZ, 2, spectral)

    def along_z(p):
        rows = dot3(split(work[pair_rows(p), :]), both(zb_ref, 0), TN)
        near = near_ref[:, :, lanes(p)]
        out_ref[:, :, lanes(p)] = rows.reshape(near.shape) - near

    loop(PAIRS, 4, along_z)


def call(kernel, out_shape, scratch, cost, *operands):
    return pl.pallas_call(
        kernel,
        out_shape=out_shape,
        in_specs=[pl.BlockSpec(memory_space=pltpu.VMEM)] * len(operands),
        out_specs=jax.tree.map(lambda _: pl.BlockSpec(memory_space=pltpu.VMEM), out_shape),
        scratch_shapes=scratch,
        compiler_params=pltpu.CompilerParams(vmem_limit_bytes=48 * 2**20),
        cost_estimate=pl.CostEstimate(flops=cost, bytes_accessed=8 * 2**20, transcendentals=0),
    )(*operands)


def body(base, state, wavenumber, cutoff):
    base, state = base[0], state[0, 0]
    slab_rows = base.shape[1]
    half = slab_rows // lax.axis_size("comp")
    slabs = lax.axis_size("slab")
    segs = lax.axis_size("seg")
    slab = lax.axis_index("slab")
    side = lax.axis_index("comp")
    width = 3 * slab_rows
    which = cutoff - LOW

    route = [((s, 0), ((s - 1) % segs, 0)) for s in range(segs)]
    route += [((s, 1), ((s + 1) % segs, 1)) for s in range(segs)]
    route = [(a * 2 + b, c * 2 + d) for (a, b), (c, d) in route]
    near_state = lax.ppermute(state, ("seg", "comp"), route)
    base_half = lax.dynamic_slice_in_dim(base, side * half, half, 1)
    near_base = lax.ppermute(base_half, "seg", [((s + 1) % segs, s) for s in range(segs)])

    wz = lax.dynamic_index_in_dim(jnp.asarray(z_tables()), which[2], 0, False)
    wy = lax.dynamic_index_in_dim(jnp.asarray(y_tables()), which[1], 0, False)
    filters, ahead = jnp.asarray(x_filters(slabs)), jnp.asarray(x_tables(slabs))
    pick = lambda t: lax.dynamic_slice(
        t, (which[0], slab) + (0,) * (t.ndim - 2), (1, 1) + t.shape[2:]
    )[0, 0]
    pd, xt = pick(filters), pick(ahead)
    xb = lax.dynamic_index_in_dim(jnp.asarray(x_back(slabs)), slab, 0, False)
    yb, zb = jnp.asarray(y_back()), jnp.asarray(z_back())

    modes = jax.ShapeDtypeStruct((KZ, 2 * MP, width), f32)
    spectrum = jax.ShapeDtypeStruct((KZ, MP, 384), f32)
    work = pltpu.VMEM((2 * N * KP, width), f32)
    own = call(base_ahead, modes, [work], 10**9, base, wz, wy)
    if slabs == 2:
        other = lax.ppermute(own, "slab", [(0, 1), (1, 0)])
        first = slab == 0
        got = jnp.stack([own, other])
        pd = jnp.where(first, pd, pd[:, ::-1])
    else:
        got = lax.all_gather(own, "slab")
    g, f = call(flux_ahead, (modes, modes), [work] * 3, 4 * 10**9, base, state, wz, wy)

    y = jnp.arange(N, dtype=jnp.int32)
    phase = jnp.mod(wavenumber[0] * y, N).astype(f32) * (2.0 * jnp.pi / N)
    force = jnp.repeat(forcing_amp * jnp.sin(phase), N)[None]
    state_modes, base_modes = call(
        functools.partial(gradients, slabs), (spectrum, spectrum), [work] * 3, 8 * 10**9,
        got, base, state, force, pd, yb, zb, wz, wy, xt, g, f,
    )
    if slabs == 2:
        swap = lambda v: lax.ppermute(v, "slab", [(0, 1), (1, 0)])
        state_parts = (state_modes, swap(state_modes))
        base_parts = (base_modes, swap(base_modes))
    else:
        state_parts = (lax.psum(state_modes, "slab"),)
        base_parts = (lax.psum(base_modes, "slab"),)

    shape = jax.ShapeDtypeStruct(base.shape, f32)
    last = functools.partial(finish, len(state_parts))
    near_wide = jnp.concatenate([near_base, near_base], axis=1)
    base_gap = call(last, shape, [work], 10**9, *base_parts, near_wide, xb, yb, zb)
    base_gap = lax.dynamic_slice_in_dim(base_gap, side * half, half, 1)
    state_gap = call(last, shape, [work], 10**9, *state_parts, near_state, xb, yb, zb)
    return base_gap[None], state_gap[None, None]


def solution(mesh):
    return jax.shard_map(
        body,
        mesh=mesh,
        in_specs=(
            P(("groups", "seg"), None, "slab", None),
            P(("groups", "seg"), "comp", None, "slab", None),
            P("groups"),
            P("groups"),
        ),
        out_specs=(
            P(("groups", "seg"), None, ("slab", "comp"), None),
            P(("groups", "seg"), "comp", None, "slab", None),
        ),
        check_vma=False,
    )
```

time: 490 us -> 162 us (0.33); the launches traced: 483 us -> 162 us
  other arithmetic: 145 us -> 3.67 us
  matrix products: 137 us -> 0 us
  local copies, waits for them, and re-layouts: 124 us -> 8.91 us
  Pallas kernels: 0 us -> 75.5 us
  starting transfers between devices: 37 us -> 9.38 us
  waiting for transfers between devices: 35 us -> 56.9 us
    dot_general x21 -> x0, matrix products: 137 us -> none  [the longest x4 30.7 us: yz_forward(): jnp.einsum('sry,...yk->s...rk', forward_transform_y, along_z, precision=h...]
    pallas_call x0 -> x5, Pallas kernels: none -> 75.5 us  [call(): pl.pallas_call(kernel, out_shape=out_shape, in_specs=[pl.BlockSpec(memory...]
    ppermute x4 -> x5, waiting for transfers between devices: 0.23 us -> 56.9 us  [the longest x2 31.8 us: body(): swap = lambda v: lax.ppermute(v, 'slab', [(0, 1), (1, 0)])]
    unnamed x154 -> x20, local copies, waits for them, and re-layouts: 57.1 us -> 4.02 us
    sub x21 -> x1, other arithmetic: 50.4 us -> 0.66 us  [body(): which = cutoff - LOW]
    all_to_all x7 -> x0, other arithmetic: 43 us -> none  [the longest x2 20.8 us: spectral(): lax.all_to_all(state_modes, ('slab', 'comp'), split_axis=4, concat_axis=2...]
    all_to_all x7 -> x0, waiting for transfers between devices: 34.8 us -> none  [the longest x1 16.7 us: body(): lax.all_to_all(grad_spread, ('slab', 'comp'), split_axis=1, concat_axis=3...]
    all_to_all x7 -> x0, starting transfers between devices: 30.4 us -> none  [the longest x2 8.65 us: spectral(): lax.all_to_all(state_modes, ('slab', 'comp'), split_axis=4, concat_axis=2...]
  transfers between devices with their start and end apart: 11 -> 5, of which waited for: 5 -> 5; matrix products, arithmetic and copies ran while one was open for 59% -> 2% of each run, Pallas kernels for 0% -> 15%
where the time goes in v1:
time: 162 us
  Pallas kernels  75.5 us (47%)
  waiting for transfers between devices  56.9 us (35%)
  starting transfers between devices  9.38 us (6%)
  local copies, waits for them, and re-layouts  8.91 us (6%)
  between operations  7.35 us (5%)
  other arithmetic  3.67 us (2%)
    pallas_call x5, Pallas kernels, call(): pl.pallas_call(kernel, out_shape=out_shape, in_specs=[pl.BlockSpec(memory...  75.5 us
    ppermute x2, waiting for transfers between devices, body(): swap = lambda v: lax.ppermute(v, 'slab', [(0, 1), (1, 0)])  31.8 us
    ppermute x1, waiting for transfers between devices, body(): lax.ppermute(base_half, 'seg', [((s + 1) % segs, s) for s in range(segs)])  17 us
    ppermute x1, waiting for transfers between devices, body(): other = lax.ppermute(own, 'slab', [(0, 1), (1, 0)])  5.52 us
    unnamed x20, local copies, waits for them, and re-layouts  4.02 us
    ppermute x1, starting transfers between devices, body(): lax.ppermute(base_half, 'seg', [((s + 1) % segs, s) for s in range(segs)])  3.65 us
  transfers between devices with their start and end apart: 5, of which 5 were waited for; matrix products, arithmetic and copies ran while one was open for 2% of the time, Pallas kernels for 15%

profile of v1, /device:TPU:0, one launch (start us, length us, event | category | flops | bytes accessed | tf_op | source)
XLA Modules:
  0.0 161.7 jit_solution(16863573217227767972)
XLA Ops:
  0.6 0.7 broadcast_add_fusion
  1.3 0.7 fusion.5
  6.0 1.0 dynamic-slice_bitcast_fusion.5
  6.9 0.0 copy-start.3
  6.9 1.4 copy-done.3
  8.3 4.8 %shard_map.122 = f32[22,96,96]{2,1,0:T(8,128)S(1)} custom-call(f32[3,32,4096]{2,1,0:T(8,128)S(1)} %bitcast.25, bf16[2,2,96,128]{3,2,1,0:T(8,128)(2,1)S(1)} %get-tuple-element.14.wz_ref, bf16[2,2,96,128]{3,2,1,0:T(8,128)(2,1)S(1)} %get-tuple-element.13.wy_ref), custom_call_target="tpu_custom_call" | custom-call | flops 1000000000 | bytes 8388608 | tf_op jit(solution)/shard_map/pallas_call | solution.py:355
  13.1 0.0 copy-start.4
  13.1 3.0 %collective-permute-start = (f32[22,96,96]{2,1,0:T(8,128)S(1)}, f32[22,96,96]{2,1,0:T(8,128)}, u32[]{:S(2)}, u32[]{:S(2)}) collective-permute-start(f32[22,96,96]{2,1,0:T(8,128)S(1)} %shard_map.122), channel_id=1, source_target_pairs={{0,2},{2,0},{1,3},{3,1},{4,6},{6,4},{5,7},{7,5},{8,10},{10,8},{9,1... | collective-permute-start | bytes 2433032 | tf_op jit(solution)/shard_map/ppermute | solution.py:399
  18.1 0.1 fusion.3
  18.2 0.1 broadcast_in_dim.9
  18.2 0.1 broadcast_in_dim_reshape.3.force_ref
  19.0 0.9 dynamic-slice_bitcast_fusion.4
  19.9 1.1 dynamic-slice_bitcast_fusion.2.xt_ref
  21.1 0.0 copy-done.4
  21.1 0.0 copy-start.6
  21.1 1.4 copy-done.6
  22.5 12.0 %shard_map.123 = (f32[22,96,96]{2,1,0:T(8,128)S(1)}, f32[22,96,96]{2,1,0:T(8,128)S(1)}) custom-call(f32[3,32,4096]{2,1,0:T(8,128)S(1)} %bitcast.26, f32[3,32,4096]{2,1,0:T(8,128)S(1)} %bitcast.29, bf16[2,2,96,128]{3,2,1,0:T(8,128)(2,1)S(1)} %get-tuple-element.14.wz_ref, bf16[2,2,96,128]{3,2,1,0:T(8,128)(2,1)S(1)} %get-tuple-element.13.wy_ref), custom_call_target="tpu_custom_call" | custom-call | flops 4000000000 | bytes 8388608 | tf_op jit(solution)/shard_map/pallas_call | solution.py:355
  34.6 5.5 %collective-permute-done = f32[22,96,96]{2,1,0:T(8,128)} collective-permute-done((f32[22,96,96]{2,1,0:T(8,128)S(1)}, f32[22,96,96]{2,1,0:T(8,128)}, u32[]{:S(2)}, u32[]{:S(2)}) %collective-permute-start) | collective-permute-done | bytes 811040 | tf_op jit(solution)/shard_map/ppermute | solution.py:399
  40.1 0.0 copy-start.2
  40.1 0.0 copy-start.5
  40.1 2.8 %pad_maximum_fusion.got_ref = f32[2,22,96,96]{3,2,1,0:T(8,128)} fusion(f32[1,22,96,96]{3,2,1,0:T(8,128)} %bitcast.6, f32[1,22,96,96]{3,2,1,0:T(8,128)S(1)} %bitcast.24), kind=kLoop, calls=%fused_computation | loop fusion | flops 405504 | bytes 3244032 | tf_op jit(solution)/shard_map/stack | solution.py:401
  42.9 0.0 copy-done.2
  42.9 0.0 copy-done.5
  42.9 0.0 copy-start.9
  42.9 36.2 %shard_map.124 = (f32[22,48,384]{2,1,0:T(8,128)}, f32[22,48,384]{2,1,0:T(8,128)}) custom-call(f32[2,22,96,96]{3,2,1,0:T(8,128)} %pad_maximum_fusion.got_ref, f32[3,32,4096]{2,1,0:T(8,128)S(1)} %bitcast.27, f32[3,32,4096]{2,1,0:T(8,128)} %bitcast.28, f32[1,4096]{1,0:T(1,128)S(1)} %broadcast_in_dim_reshape.3.force_ref, ...), custom_call_target="tpu_custom_call" | custom-call | flops 8000000000 | bytes 8388608 | tf_op jit(solution)/shard_map/pallas_call | solution.py:355
  79.1 0.0 copy-start.7
  79.1 1.7 %collective-permute-start.1 = (f32[22,48,384]{2,1,0:T(8,128)}, f32[22,48,384]{2,1,0:T(8,128)S(1)}, u32[]{:S(2)}, u32[]{:S(2)}) collective-permute-start(f32[22,48,384]{2,1,0:T(8,128)} %get-tuple-element.8.refs_0_), channel_id=1, source_target_pairs={{0,2},{2,0},{1,3},{3,1},{4,6},{6,4},{5,7},{7,5},{8,10},{10,8},{9,1... | collective-permute-start | bytes 4866056 | tf_op jit(solution)/shard_map/ppermute | solution.py:415
  80.8 0.1 dynamic-slice_bitcast_fusion.1
  80.9 3.6 %collective-permute-start.2 = (f32[3,16,4096]{2,1,0:T(8,128)S(1)}, f32[3,16,4096]{2,1,0:T(8,128)S(1)}, u32[]{:S(2)}, u32[]{:S(2)}) collective-permute-start(f32[3,16,4096]{2,1,0:T(8,128)S(1)} %dynamic-slice_bitcast_fusion.1), channel_id=1, source_target_pairs={{4,0},{8,4},{12,8},{0,12},{5,1},{9,5},{13,9},{1,13},{6,2},{10,6},{... | collective-permute-start | bytes 2359304 | tf_op jit(solution)/shard_map/ppermute | solution.py:382
  84.5 0.0 copy-start.1
  84.5 0.5 collective-permute-start.3
  85.1 0.0 copy-done.7
  85.1 0.4 collective-permute-start.4
  85.5 0.0 copy-done.9
  85.6 17.0 %collective-permute-done.2 = f32[3,16,4096]{2,1,0:T(8,128)S(1)} collective-permute-done((f32[3,16,4096]{2,1,0:T(8,128)S(1)}, f32[3,16,4096]{2,1,0:T(8,128)S(1)}, u32[]{:S(2)}, u32[]{:S(2)}) %collective-permute-start.2) | collective-permute-done | bytes 786464 | tf_op jit(solution)/shard_map/ppermute | solution.py:382
  102.5 0.1 pad_maximum_fusion.1.refs_2_
  102.7 15.0 %collective-permute-done.1.refs_1_ = f32[22,48,384]{2,1,0:T(8,128)S(1)} collective-permute-done((f32[22,48,384]{2,1,0:T(8,128)}, f32[22,48,384]{2,1,0:T(8,128)S(1)}, u32[]{:S(2)}, u32[]{:S(2)}) %collective-permute-start.1) | collective-permute-done | bytes 1622048 | tf_op jit(solution)/shard_map/ppermute | solution.py:415
  117.7 0.0 copy-start.8
  117.7 1.2 copy-done.8
  118.9 0.0 copy-done.1
  118.9 0.0 copy-start
  118.9 11.4 %shard_map.125 = f32[3,32,4096]{2,1,0:T(8,128)S(1)} custom-call(f32[22,48,384]{2,1,0:T(8,128)S(1)} %copy-done.1, f32[22,48,384]{2,1,0:T(8,128)} %copy-done.8, f32[3,32,4096]{2,1,0:T(8,128)S(1)} %pad_maximum_fusion.1.refs_2_, bf16[2,2,384,96]{3,2,1,0:T(8,128)(2,1)S(1)} %dynamic-slice_bitcast_fusion.3.refs_3_, bf16[2,2,128,96]{3,2,1,0:T(8,128)(2,1)S(1)} %copy-done.2, ...), custom_call_target="tpu_custom_call" | custom-call | flops 1000000000 | bytes 8388608 | tf_op jit(solution)/shard_map/pallas_call | solution.py:355
  130.3 0.9 dynamic-slice_bitcast_fusion
  131.3 2.7 %collective-permute-done.4.refs_2_ = f32[3,32,4096]{2,1,0:T(8,128)S(1)} collective-permute-done((f32[3,32,4096]{2,1,0:T(8,128)S(1)}, f32[3,32,4096]{2,1,0:T(8,128)S(1)}, u32[]{:S(2)}, u32[]{:S(2)}) %collective-permute-start.4) | collective-permute-done | bytes 1572896 | tf_op jit(solution)/shard_map/ppermute | solution.py:380
  134.0 16.7 %collective-permute-done.3.refs_1_ = f32[22,48,384]{2,1,0:T(8,128)S(1)} collective-permute-done((f32[22,48,384]{2,1,0:T(8,128)}, f32[22,48,384]{2,1,0:T(8,128)S(1)}, u32[]{:S(2)}, u32[]{:S(2)}) %collective-permute-start.3) | collective-permute-done | bytes 1622048 | tf_op jit(solution)/shard_map/ppermute | solution.py:415
  150.7 0.0 copy-done
  150.7 11.0 %shard_map.126 = f32[3,32,4096]{2,1,0:T(8,128)} custom-call(f32[22,48,384]{2,1,0:T(8,128)S(1)} %copy-done, f32[22,48,384]{2,1,0:T(8,128)S(1)} %collective-permute-done.3.refs_1_, f32[3,32,4096]{2,1,0:T(8,128)S(1)} %collective-permute-done.4.refs_2_, bf16[2,2,384,96]{3,2,1,0:T(8,128)(2,1)S(1)} %dynamic-slice_bitcast_fusion.3.refs_3_, ...), custom_call_target="tpu_custom_call" | custom-call | flops 1000000000 | bytes 8388608 | tf_op jit(solution)/shard_map/pallas_call | solution.py:355
  (2 shorter events, 0.1 us)
Async XLA Ops:
  6.9 1.4 copy-start.3
  13.1 8.0 %copy-start.4 = (f32[1,3,32,4096]{3,2,1,0:T(8,128)S(1)}, f32[1,3,32,4096]{3,2,1,0:T(8,128)}, u32[]{:S(2)}) copy-start(f32[1,3,32,4096]{3,2,1,0:T(8,128)} %param.11) | copy-start | bytes 4718596
  13.1 27.0 %collective-permute-start = (f32[22,96,96]{2,1,0:T(8,128)S(1)}, f32[22,96,96]{2,1,0:T(8,128)}, u32[]{:S(2)}, u32[]{:S(2)}) collective-permute-start(f32[22,96,96]{2,1,0:T(8,128)S(1)} %shard_map.122), channel_id=1, source_target_pairs={{0,2},{2,0},{1,3},{3,1},{4,6},{6,4},{5,7},{7,5},{8,10},{10,8},{9,1... | collective-permute-start | bytes 2433032 | tf_op jit(solution)/shard_map/ppermute | solution.py:399
  21.1 1.4 copy-start.6
  40.1 2.8 %copy-start.2 = (bf16[2,2,128,96]{3,2,1,0:T(8,128)(2,1)S(1)}, bf16[2,2,128,96]{3,2,1,0:T(8,128)(2,1)}, u32[]{:S(2)}) copy-start(bf16[2,2,128,96]{3,2,1,0:T(8,128)(2,1)} %constant.67.clone.yb_ref.refs_4_) | copy-start | bytes 294916
  40.1 2.8 %copy-start.5 = (bf16[2,2,96,128]{3,2,1,0:T(8,128)(2,1)S(1)}, bf16[2,2,96,128]{3,2,1,0:T(8,128)(2,1)}, u32[]{:S(2)}) copy-start(bf16[2,2,96,128]{3,2,1,0:T(8,128)(2,1)} %constant.68.clone.zb_ref.refs_5_) | copy-start | bytes 294916
  42.9 42.6 %copy-start.9 = (bf16[2,2,2,384,96]{4,3,2,1,0:T(8,128)(2,1)S(1)}, bf16[2,2,2,384,96]{4,3,2,1,0:T(8,128)(2,1)}, u32[]{:S(2)}) copy-start(bf16[2,2,2,384,96]{4,3,2,1,0:T(8,128)(2,1)} %constant.66.clone) | copy-start | bytes 1769476
  79.1 6.0 %copy-start.7 = (f32[1,1,3,32,4096]{4,3,2,1,0:T(8,128)S(1)}, f32[1,1,3,32,4096]{4,3,2,1,0:T(8,128)}, u32[]{:S(2)}) copy-start(f32[1,1,3,32,4096]{4,3,2,1,0:T(8,128)} %param.12) | copy-start | bytes 4718596
  79.1 38.6 %collective-permute-start.1 = (f32[22,48,384]{2,1,0:T(8,128)}, f32[22,48,384]{2,1,0:T(8,128)S(1)}, u32[]{:S(2)}, u32[]{:S(2)}) collective-permute-start(f32[22,48,384]{2,1,0:T(8,128)} %get-tuple-element.8.refs_0_), channel_id=1, source_target_pairs={{0,2},{2,0},{1,3},{3,1},{4,6},{6,4},{5,7},{7,5},{8,10},{10,8},{9,1... | collective-permute-start | bytes 4866056 | tf_op jit(solution)/shard_map/ppermute | solution.py:415
  80.9 21.6 %collective-permute-start.2 = (f32[3,16,4096]{2,1,0:T(8,128)S(1)}, f32[3,16,4096]{2,1,0:T(8,128)S(1)}, u32[]{:S(2)}, u32[]{:S(2)}) collective-permute-start(f32[3,16,4096]{2,1,0:T(8,128)S(1)} %dynamic-slice_bitcast_fusion.1), channel_id=1, source_target_pairs={{4,0},{8,4},{12,8},{0,12},{5,1},{9,5},{13,9},{1,13},{6,2},{10,6},{... | collective-permute-start | bytes 2359304 | tf_op jit(solution)/shard_map/ppermute | solution.py:382
  84.5 34.3 %copy-start.1 = (f32[22,48,384]{2,1,0:T(8,128)S(1)}, f32[22,48,384]{2,1,0:T(8,128)}, u32[]{:S(2)}) copy-start(f32[22,48,384]{2,1,0:T(8,128)} %get-tuple-element.8.refs_0_) | copy-start | bytes 4866052
  84.5 66.2 %collective-permute-start.3 = (f32[22,48,384]{2,1,0:T(8,128)}, f32[22,48,384]{2,1,0:T(8,128)S(1)}, u32[]{:S(2)}, u32[]{:S(2)}) collective-permute-start(f32[22,48,384]{2,1,0:T(8,128)} %get-tuple-element.9.refs_0_), channel_id=1, source_target_pairs={{0,2},{2,0},{1,3},{3,1},{4,6},{6,4},{5,7},{7,5},{8,10},{10,8},{9,1... | collective-permute-start | bytes 4866056 | tf_op jit(solution)/shard_map/ppermute | solution.py:415
  85.1 48.9 %collective-permute-start.4 = (f32[3,32,4096]{2,1,0:T(8,128)S(1)}, f32[3,32,4096]{2,1,0:T(8,128)S(1)}, u32[]{:S(2)}, u32[]{:S(2)}) collective-permute-start(f32[3,32,4096]{2,1,0:T(8,128)S(1)} %bitcast.30), channel_id=1, source_target_pairs={{0,12},{4,0},{8,4},{12,8},{1,5},{5,9},{9,13},{13,1},{2,14},{6,2},{... | collective-permute-start | bytes 4718600 | tf_op jit(solution)/shard_map/ppermute | solution.py:380
  117.7 1.2 copy-start.8
  118.9 31.8 %copy-start = (f32[22,48,384]{2,1,0:T(8,128)S(1)}, f32[22,48,384]{2,1,0:T(8,128)}, u32[]{:S(2)}) copy-start(f32[22,48,384]{2,1,0:T(8,128)} %get-tuple-element.9.refs_0_) | copy-start | bytes 4866052

commit v2 on v1

v2 whole, which is shorter than its diff:
```python
import functools

import jax
import jax.numpy as jnp
import ml_dtypes
import numpy as np
from jax import lax
from jax.experimental import pallas as pl
from jax.experimental.pallas import tpu as pltpu
from jax.sharding import PartitionSpec as P

N = 64
BACK, GRID, AHEAD, SPEC, Z1, Z2, Z3, Y1 = 4, 4, 4, 4, 8, 4, 8, 6
THIRD = N // 3
LOW = THIRD - 3
KZ = THIRD + 1
KP = 24
MP = 48
PAIRS = N // 2
FLUX = 14 * 10**9
HALF = KZ // 2
viscosity = 0.025
time_step = 0.02
forcing_amp = 10.0
f32 = jnp.float32
bf16 = jnp.bfloat16

NN = (((1,), (0,)), ((), ()))
NT = (((1,), (1,)), ((), ()))


def split(value):
    high = value.astype(bf16)
    return high, (value - high.astype(f32)).astype(bf16)


def dot3(left, right, dims):
    dot = functools.partial(lax.dot_general, dimension_numbers=dims, preferred_element_type=f32)
    return dot(left[0], right[0]) + (dot(left[0], right[1]) + dot(left[1], right[0]))


def table(values):
    values = np.asarray(values, np.float32)
    high = values.astype(ml_dtypes.bfloat16)
    low = (values - high.astype(np.float32)).astype(ml_dtypes.bfloat16)
    return np.stack([high, low], axis=-3)


def table3(values):
    high, low = np.moveaxis(table(values), -3, 0)
    return np.concatenate([high, high, low], axis=-1)


def left3(left, value, dims):
    high, low = split(value)
    deep = jnp.concatenate([high, low, high], axis=dims[0][1][0])
    return lax.dot_general(left, deep, dimension_numbers=dims, preferred_element_type=f32)


def signed():
    m = np.arange(2 * THIRD + 1)
    return np.where(m <= THIRD, m, m - (2 * THIRD + 1))


def angles(first, second):
    return np.mod(np.outer(first, second), N) * (2 * np.pi / N)


def cuts():
    return range(LOW, THIRD + 1)


def z_tables():
    plain, ik = [], []
    k = np.arange(KZ)
    a = angles(k, np.arange(N))
    for cut in cuts():
        keep = 1.0 * (k <= cut)[:, None]
        w = np.zeros((2, KP, N))
        v = np.zeros((2, KP, N))
        w[0, :KZ], w[1, :KZ] = keep * np.cos(a), -keep * np.sin(a)
        v[0, :KZ], v[1, :KZ] = keep * k[:, None] * np.sin(a), keep * k[:, None] * np.cos(a)
        plain.append(np.kron(np.eye(2), w.reshape(2 * KP, N)))
        ik.append(np.kron(np.eye(2), v.reshape(2 * KP, N)))
    return table3(np.stack([np.stack(plain), np.stack(ik)], axis=1))


def y_tables():
    out = []
    m = signed()
    count = len(m)
    a = angles(m, np.arange(N))
    for cut in cuts():
        keep = 1.0 * (np.abs(m) <= cut)[:, None]
        c, s = keep * np.cos(a), keep * np.sin(a)
        w = np.zeros((2, MP, N, 2))
        w[0, :count, :, 0], w[0, :count, :, 1] = c, s
        w[1, :count, :, 0], w[1, :count, :, 1] = -s, c
        v = np.zeros_like(w)
        v[0, :count] = -m[:, None, None] * w[1, :count]
        v[1, :count] = m[:, None, None] * w[0, :count]
        out.append(np.stack([w.reshape(2 * MP, 2 * N), v.reshape(2 * MP, 2 * N)]))
    return table3(np.stack(out))


def y_back():
    m = signed()
    count = len(m)
    a = angles(np.arange(N), m)
    c, s = np.cos(a) / N, np.sin(a) / N
    w = np.zeros((N, 2, 2, MP))
    w[:, 0, 0, :count], w[:, 0, 1, :count] = c, -s
    w[:, 1, 0, :count], w[:, 1, 1, :count] = s, c
    v = np.zeros_like(w)
    v[:, :, 0, :count] = m * w[:, :, 1, :count]
    v[:, :, 1, :count] = -m * w[:, :, 0, :count]
    return table3(np.stack([w.reshape(2 * N, 2 * MP), v.reshape(2 * N, 2 * MP)]))


def z_back():
    k = np.arange(KZ)
    a = angles(k, np.arange(N))
    weight = (np.where(k == 0, 1.0, 2.0) / N)[:, None]
    w = np.zeros((2, KP, N))
    w[0, :KZ], w[1, :KZ] = weight * np.cos(a), -weight * np.sin(a)
    v = np.zeros_like(w)
    v[0, :KZ] = k[:, None] * w[1, :KZ]
    v[1, :KZ] = -k[:, None] * w[0, :KZ]
    pair = lambda t: np.kron(np.eye(2), t.reshape(2 * KP, N))
    return table3(np.stack([pair(w).T, pair(v).T]))


def x_filters(slabs):
    rows = N // slabs
    out = []
    x = np.arange(N)
    for cut in cuts():
        n = np.arange(-cut, cut + 1)
        d = np.mod(x[:, None] - x[None, :], N)
        phase = 2 * np.pi / N * n[:, None, None] * -d
        plain = np.cos(phase).sum(0) / N
        deriv = (-n[:, None, None] * np.sin(phase)).sum(0) / N
        both = np.stack([plain, deriv]).reshape(2, slabs, rows, slabs, rows)
        wide = np.zeros((slabs, 2, slabs, 3, rows, 3, rows))
        for i in range(3):
            wide[:, :, :, i, :, i, :] = both.transpose(3, 0, 1, 2, 4)
        out.append(wide.reshape(slabs, 2, slabs, 3 * rows, 3 * rows))
    return table(np.stack(out))


def x_tables(slabs):
    rows = N // slabs
    n = signed()
    count = len(n)
    a = angles(np.arange(N), n).reshape(slabs, rows, count)
    out = []
    for cut in cuts():
        keep = 1.0 * (np.abs(n) <= cut)
        c, s = np.cos(a) * keep, np.sin(a) * keep
        w = np.zeros((slabs, 2, 2, 3, rows, 3, 2, 64))
        for i in range(3):
            w[:, 0, 0, i, :, i, 0, :count] = c
            w[:, 0, 0, i, :, i, 1, :count] = -s
            w[:, 0, 1, i, :, i, 0, :count] = s
            w[:, 0, 1, i, :, i, 1, :count] = c
        w[:, 1, :, :, :, :, 0, :count] = -n * w[:, 0, :, :, :, :, 1, :count]
        w[:, 1, :, :, :, :, 1, :count] = n * w[:, 0, :, :, :, :, 0, :count]
        out.append(w.reshape(slabs, 2, 2, 3 * rows, 384))
    return table(np.stack(out))


def x_back(slabs):
    rows = N // slabs
    n = signed()
    count = len(n)
    a = angles(n, np.arange(N)).reshape(count, slabs, rows).transpose(1, 0, 2)
    c, s = np.cos(a) / N, np.sin(a) / N
    w = np.zeros((slabs, 2, 3, 2, 64, 3, rows))
    for i in range(3):
        w[:, 0, i, 0, :count, i] = c
        w[:, 0, i, 1, :count, i] = -s
        w[:, 1, i, 0, :count, i] = s
        w[:, 1, i, 1, :count, i] = c
    return table(w.reshape(slabs, 2, 384, 3 * rows))


def both(ref, *index):
    return ref[(*index, 0)], ref[(*index, 1)]


def lanes(p):
    return pl.ds(pl.multiple_of(p * 128, 128), 128)


def pair_rows(p):
    return pl.ds(pl.multiple_of(p * 4 * KP, 8), 4 * KP)


def column(k):
    return pl.ds(k, 2 * N, stride=KP)


def flat(block):
    return block.reshape(block.shape[0] * block.shape[1], block.shape[2])


def loop(count, unroll, step):
    def go(i, carry):
        step(i)
        return carry

    lax.fori_loop(0, count, go, 0, unroll=unroll)


def clear_padding(*works):
    for k in range(KZ, KP):
        for work in works:
            work[column(k), :] = jnp.zeros((2 * N, work.shape[1]), f32)


def base_ahead(base_ref, wz_ref, wy_ref, out_ref, half_ref, work):
    def along_z(p):
        work[pair_rows(p), :] = left3(wz_ref[0], flat(base_ref[:, :, lanes(p)]), NT)

    loop(PAIRS, Z1, along_z)

    def along_y(k):
        out_ref[k] = left3(wy_ref[0], work[column(k), :], NN)

    loop(KZ, Y1, along_y)
    first = HALF * lax.axis_index("comp")

    def share(j):
        half_ref[j] = out_ref[first + j]

    loop(HALF, 1, share)


def sign_step():
    return jnp.where(lax.axis_index("comp") == 0, -time_step, time_step).astype(f32)


def flux_ahead(base_ref, state_ref, wz_ref, wy_ref, g_ref, work_a, work_b):
    scale = sign_step()

    def along_z(p):
        state = state_ref[:, :, lanes(p)]
        scaled = state * scale
        f1, f2 = (flat(scaled * base_ref[j, :, lanes(p)][None]) for j in (1, 2))
        plain = wz_ref[0]
        work_a[pair_rows(p), :] = left3(plain, flat(state), NT) + left3(wz_ref[1], f2, NT)
        work_b[pair_rows(p), :] = left3(plain, f1, NT)

    loop(PAIRS, Z2, along_z)

    def along_y(k):
        g_ref[k] = left3(wy_ref[0], work_a[column(k), :], NN) + left3(
            wy_ref[1], work_b[column(k), :], NN
        )

    loop(KZ, Y1, along_y)


def flux_x_ahead(base_ref, state_ref, wz_ref, wy_ref, f_ref, work):
    scale = sign_step()

    def along_z(p):
        f0 = flat(state_ref[:, :, lanes(p)] * scale * base_ref[0, :, lanes(p)][None])
        work[pair_rows(p), :] = left3(wz_ref[0], f0, NT)

    loop(PAIRS, Z2, along_z)

    def along_y(k):
        f_ref[k] = left3(wy_ref[0], work[column(k), :], NN)

    loop(KZ, Y1, along_y)


def gradients(
    slabs, count, *refs,
):
    got, rest = refs[:count], refs[count:]
    side = lax.axis_index("comp")
    if count == 1:
        visits = [(lambda j: (j, [got[0][s, j] for s in range(slabs)]), KZ)]
    else:
        own, mine, partner = got

        def visit(ref, first):
            return lambda j: (first + j, [own[first + j], ref[j]])

        visits = [
            (visit(mine, HALF * side), HALF),
            (visit(partner, HALF * (1 - side)), HALF),
        ]
    gradients_of(slabs, visits, *rest)


def gradients_of(
    slabs, visits, base_ref, state_ref, force_ref, pd_ref, yb_ref, zb_ref, wz_ref, wy_ref,
    xt_ref, base_out_ref, coupled_ref, work_0, work_1, work_2,
):
    tangent = lax.axis_index("comp") == 0

    def back_y(visit, j):
        k, sources = visit(j)
        sources = [split(source) for source in sources]

        def across(kind):
            total = dot3(sources[0], both(pd_ref, kind, 0), NN)
            for s in range(1, slabs):
                total = total + dot3(sources[s], both(pd_ref, kind, s), NN)
            return total

        plain, deriv = across(0), across(1)
        work_0[column(k), :] = left3(yb_ref[0], deriv, NN)
        work_1[column(k), :] = left3(yb_ref[1], plain, NN)
        work_2[column(k), :] = left3(yb_ref[0], plain, NN)

    clear_padding(work_0, work_1, work_2)
    for visit, count in visits:
        loop(count, BACK, functools.partial(back_y, visit))

    def grid_space(p):
        state = state_ref[:, :, lanes(p)]
        base = base_ref[:, :, lanes(p)]
        grad = []
        for work, kind in ((work_0, 0), (work_1, 0), (work_2, 1)):
            rows = left3(zb_ref[kind], work[pair_rows(p), :], NN).T
            grad.append(rows.reshape(base.shape))
        coupled, driven = [], []
        for i in range(3):
            total = 0.0
            drive = 0.0
            for j in range(3):
                total = total + jnp.where(tangent, grad[j][i], grad[i][j]) * state[j]
                drive = drive + grad[j][i] * base[j]
            if i == 0:
                drive = drive - force_ref[:, lanes(p)]
            coupled.append(-time_step * total)
            driven.append(base[i] - time_step * drive)
        plain = wz_ref[0]
        coupled_ref[pair_rows(p), :] = left3(plain, jnp.concatenate(coupled, axis=0), NT)
        work_1[pair_rows(p), :] = left3(plain, jnp.concatenate(driven, axis=0), NT)

    loop(PAIRS, GRID, grid_space)

    waves = plane_waves()
    first = HALF * lax.axis_index("comp")

    def base_ahead_x(step):
        j = HALF - 1 - step
        k = first + j
        driven = left3(wy_ref[0], work_1[column(k), :], NN)
        modes = 0.0
        for d in range(2):
            rows = slice(d * MP, (d + 1) * MP)
            modes = modes + dot3(split(driven[rows]), both(xt_ref, 0, d), NN)
        emit(waves, base_out_ref, j, HALF, modes, k)

    loop(HALF, AHEAD, base_ahead_x)


def emit(waves, ref, slot, last, modes, k):
    new = projected(waves, modes, k)
    ref[slot] = jnp.concatenate(new[:2], axis=1)
    ref[last] = jnp.concatenate([new[2], jnp.zeros_like(new[2])], axis=1)


def state_ahead_x(coupled_ref, wy_ref, xt_ref, g_ref, f_ref, out_ref):
    waves = plane_waves()

    def ahead_x(step):
        k = KZ - 1 - step
        total = g_ref[k] + left3(wy_ref[0], coupled_ref[column(k), :], NN)
        outer = f_ref[k]
        modes = 0.0
        for d in range(2):
            rows = slice(d * MP, (d + 1) * MP)
            modes = modes + dot3(split(total[rows]), both(xt_ref, 0, d), NN)
            modes = modes + dot3(split(outer[rows]), both(xt_ref, 1, d), NN)
        emit(waves, out_ref, k, KZ, modes, k)

    loop(KZ, AHEAD, ahead_x)


def plane_waves():
    column_n = lax.rem(lax.broadcasted_iota(jnp.int32, (MP, 128), 1), 64)
    row_m = lax.broadcasted_iota(jnp.int32, (MP, 128), 0)
    wrap = lambda v: jnp.where(v <= THIRD, v, v - (2 * THIRD + 1)).astype(f32)
    return wrap(column_n), wrap(row_m)


def projected(waves, modes, k):
    wave_x, wave_y = waves
    wave_z = jnp.asarray(k, jnp.int32).astype(f32)
    square = wave_x * wave_x + wave_y * wave_y + wave_z * wave_z
    safe = jnp.where(square > 0, square, 1.0)
    damping = 1.0 / (1.0 + viscosity * time_step * square)
    w = [modes[:, i * 128 : (i + 1) * 128] for i in range(3)]
    divergence = (wave_x * w[0] + wave_y * w[1] + wave_z * w[2]) / safe
    return [
        damping * (w[0] - wave_x * divergence),
        damping * (w[1] - wave_y * divergence),
        damping * (w[2] - wave_z * divergence),
    ]


def finish(count, halved, *refs):
    parts, (near_ref, xb_ref, yb_ref, zb_ref, out_ref, work) = refs[:count], refs[count:]
    wave_x, wave_y = plane_waves()
    clear_padding(work)

    def spectral(parts, first, last, j):
        k = first + j
        modes, third = 0.0, 0.0
        for part in parts:
            modes = modes + part[j]
            third = third + part[last, :, :128]
        w0, w1 = modes[:, :128], modes[:, 128:]
        whole = jnp.asarray(k, jnp.int32)
        inverse = 1.0 / jnp.maximum(whole, 1).astype(f32)
        w2 = jnp.where(whole == 0, third, -(wave_x * w0 + wave_y * w1) * inverse)
        new = split(jnp.concatenate([w0, w1, w2], axis=1))
        rows = [dot3(new, both(xb_ref, d), NN) for d in range(2)]
        work[column(k), :] = left3(yb_ref[0], jnp.concatenate(rows, axis=0), NN)

    if halved:
        side = lax.axis_index("comp")
        for part, place in zip(parts, (side, 1 - side)):
            loop(HALF, SPEC, functools.partial(spectral, [part], HALF * place, HALF))
    else:
        loop(KZ, SPEC, functools.partial(spectral, parts, 0, KZ))

    def along_z(p):
        rows = left3(zb_ref[0], work[pair_rows(p), :], NN).T
        near = near_ref[:, :, lanes(p)]
        out_ref[:, :, lanes(p)] = rows.reshape(near.shape) - near

    loop(PAIRS, Z3, along_z)


def call(kernel, out_shape, scratch, cost, *operands):
    return pl.pallas_call(
        kernel,
        out_shape=out_shape,
        in_specs=[pl.BlockSpec(memory_space=pltpu.VMEM)] * len(operands),
        out_specs=jax.tree.map(lambda _: pl.BlockSpec(memory_space=pltpu.VMEM), out_shape),
        scratch_shapes=scratch,
        compiler_params=pltpu.CompilerParams(vmem_limit_bytes=48 * 2**20),
        cost_estimate=pl.CostEstimate(flops=cost, bytes_accessed=2**10, transcendentals=0),
    )(*operands)


def body(base, state, wavenumber, cutoff):
    base, state = base[0], state[0, 0]
    slab_rows = base.shape[1]
    half = slab_rows // lax.axis_size("comp")
    slabs = lax.axis_size("slab")
    segs = lax.axis_size("seg")
    slab = lax.axis_index("slab")
    side = lax.axis_index("comp")
    width = 3 * slab_rows
    which = cutoff - LOW

    route = [((s, 0), ((s - 1) % segs, 0)) for s in range(segs)]
    route += [((s, 1), ((s + 1) % segs, 1)) for s in range(segs)]
    route = [(a * 2 + b, c * 2 + d) for (a, b), (c, d) in route]
    wz = lax.dynamic_index_in_dim(jnp.asarray(z_tables()), which[2], 0, False)
    wy = lax.dynamic_index_in_dim(jnp.asarray(y_tables()), which[1], 0, False)
    filters, ahead = jnp.asarray(x_filters(slabs)), jnp.asarray(x_tables(slabs))
    pick = lambda t: lax.dynamic_slice(
        t, (which[0], slab) + (0,) * (t.ndim - 2), (1, 1) + t.shape[2:]
    )[0, 0]
    pd, xt = pick(filters), pick(ahead)
    xb = lax.dynamic_index_in_dim(jnp.asarray(x_back(slabs)), slab, 0, False)
    yb, zb = jnp.asarray(y_back()), jnp.asarray(z_back())

    modes = jax.ShapeDtypeStruct((KZ, 2 * MP, width), f32)
    half_modes = jax.ShapeDtypeStruct((HALF, 2 * MP, width), f32)
    spectrum = jax.ShapeDtypeStruct((KZ + 1, MP, 256), f32)
    half_spectrum = jax.ShapeDtypeStruct((HALF + 1, MP, 256), f32)
    work = pltpu.VMEM((2 * N * KP, width), f32)
    own, share = call(base_ahead, (modes, half_modes), [work], 4 * 10**9, base, wz, wy)
    later, later_base, share = lax.optimization_barrier((state, base, share))
    near_state = lax.ppermute(later, ("seg", "comp"), route)
    base_half = lax.dynamic_slice_in_dim(later_base, side * half, half, 1)
    near_base = lax.ppermute(base_half, "seg", [((s + 1) % segs, s) for s in range(segs)])
    if slabs == 2:
        other = lax.ppermute(share, "slab", [(0, 1), (1, 0)])
        partner = lax.ppermute(other, "comp", [(0, 1), (1, 0)])
        first = slab == 0
        got = (own, other, partner)
        pd = jnp.where(first, pd, pd[:, ::-1])
    else:
        got = (lax.all_gather(own, "slab"),)
    g = call(flux_ahead, modes, [work] * 2, FLUX, base, state, wz, wy)
    f = call(flux_x_ahead, modes, [work], 10**9, base, state, wz, wy)

    *got, g, f = lax.optimization_barrier((*got, g, f))

    y = jnp.arange(N, dtype=jnp.int32)
    phase = jnp.mod(wavenumber[0] * y, N).astype(f32) * (2.0 * jnp.pi / N)
    force = jnp.repeat(forcing_amp * jnp.sin(phase), N)[None]
    lined = jax.ShapeDtypeStruct((2 * N * KP, width), f32)
    base_modes, coupled = call(
        functools.partial(gradients, slabs, len(got)), (half_spectrum, lined), [work] * 3,
        25 * 10**9, *got, base, state, force, pd, yb, zb, wz, wy, xt,
    )
    state_modes = call(state_ahead_x, spectrum, [], 3 * 10**9, coupled, wy, xt, g, f)
    near_state, near_base, state_modes = lax.optimization_barrier(
        (near_state, near_base, state_modes)
    )
    if slabs == 2:
        swap = lambda v: lax.ppermute(v, "slab", [(0, 1), (1, 0)])
        state_other = swap(state_modes)
        base_other, state_modes = lax.optimization_barrier((swap(base_modes), state_modes))
        base_sum = base_modes + base_other
        state_parts = (state_modes, state_other)
    else:
        base_sum = lax.psum(base_modes, "slab")
        state_parts = (lax.psum(state_modes, "slab"),)
    base_parts = (base_sum, lax.ppermute(base_sum, "comp", [(0, 1), (1, 0)]))

    shape = jax.ShapeDtypeStruct(base.shape, f32)
    last = functools.partial(finish, len(state_parts), False)
    last_base = functools.partial(finish, 2, True)
    near_wide = jnp.concatenate([near_base, near_base], axis=1)
    base_gap = call(last_base, shape, [work], 10**8, *base_parts, near_wide, xb, yb, zb)
    base_gap = lax.dynamic_slice_in_dim(base_gap, side * half, half, 1)
    state_gap = call(last, shape, [work], 10**10, *state_parts, near_state, xb, yb, zb)
    return base_gap[None], state_gap[None, None]


def solution(mesh):
    return jax.shard_map(
        body,
        mesh=mesh,
        in_specs=(
            P(("groups", "seg"), None, "slab", None),
            P(("groups", "seg"), "comp", None, "slab", None),
            P("groups"),
            P("groups"),
        ),
        out_specs=(
            P(("groups", "seg"), None, ("slab", "comp"), None),
            P(("groups", "seg"), "comp", None, "slab", None),
        ),
        check_vma=False,
    )
```

time: 162 us -> 117 us (0.72)
  waiting for transfers between devices: 56.9 us -> 18.2 us
  Pallas kernels: 75.5 us -> 68.4 us
  local copies, waits for them, and re-layouts: 8.91 us -> 11 us
    ppermute x1, waiting for transfers between devices: 17 us -> 0.01 us  [body(): lax.ppermute(base_half, 'seg', [((s + 1) % segs, s) for s in range(segs)])]
    ppermute x2, waiting for transfers between devices: 31.8 us -> 17.7 us  [body(): swap = lambda v: lax.ppermute(v, 'slab', [(0, 1), (1, 0)])]
    ppermute x2 -> x4, waiting for transfers between devices: 8.21 us -> 0.46 us  [the longest x1 0.45 us: body(): base_parts = (base_sum, lax.ppermute(base_sum, 'comp', [(0, 1), (1, 0)]))]
    pallas_call x5 -> x7, Pallas kernels: 75.5 us -> 68.4 us  [call(): pl.pallas_call(kernel, out_shape=out_shape, in_specs=[pl.BlockSpec(memory...]
    another operation x1 -> x0, other arithmetic: 2.79 us -> none  [body(): got = jnp.stack([own, other])]
    unnamed x20 -> x24, local copies, waits for them, and re-layouts: 4.02 us -> 4.39 us
    ppermute x2 -> x4, starting transfers between devices: 3.45 us -> 3.43 us  [the longest x1 2.93 us: body(): other = lax.ppermute(share, 'slab', [(0, 1), (1, 0)])]
  transfers between devices with their start and end apart: 5 -> 7, of which waited for: 5 -> 3; matrix products, arithmetic and copies ran while one was open for 2% -> 7% of each run, Pallas kernels for 15% -> 45%
where the time goes in v2:
time: 117 us
  Pallas kernels  68.4 us (58%)
  waiting for transfers between devices  18.2 us (16%)
  local copies, waits for them, and re-layouts  11 us (9%)
  starting transfers between devices  9.23 us (8%)
  between operations  6.98 us (6%)
  other arithmetic  3.35 us (3%)
    pallas_call x7, Pallas kernels, call(): pl.pallas_call(kernel, out_shape=out_shape, in_specs=[pl.BlockSpec(memory...  68.4 us
    ppermute x2, waiting for transfers between devices, body(): swap = lambda v: lax.ppermute(v, 'slab', [(0, 1), (1, 0)])  17.7 us
    unnamed x24, local copies, waits for them, and re-layouts  4.39 us
    ppermute x1, starting transfers between devices, body(): lax.ppermute(base_half, 'seg', [((s + 1) % segs, s) for s in range(segs)])  3.6 us
    ppermute x1, starting transfers between devices, body(): other = lax.ppermute(share, 'slab', [(0, 1), (1, 0)])  2.93 us
    squeeze x2, local copies, waits for them, and re-layouts, body(): lax.dynamic_slice(t, (which[0], slab) + (0,) * (t.ndim - 2), (1, 1) + t.s...  2.91 us
  transfers between devices with their start and end apart: 7, of which 3 were waited for; matrix products, arithmetic and copies ran while one was open for 7% of the time, Pallas kernels for 45%

profile of v2, /device:TPU:0, one launch (start us, length us, event | category | flops | bytes accessed | tf_op | source)
XLA Modules:
  0.0 117.1 jit_solution(11660189403005008674)
XLA Ops:
  0.6 0.7 broadcast_add_fusion
  1.3 0.6 fusion.5
  5.8 1.0 dynamic-slice_bitcast_fusion.4
  6.8 0.0 copy-start
  6.8 1.4 %copy-done = f32[1,3,32,4096]{3,2,1,0:T(8,128)S(1)} copy-done((f32[1,3,32,4096]{3,2,1,0:T(8,128)S(1)}, f32[1,3,32,4096]{3,2,1,0:T(8,128)}, u32[]{:S(2)}) %copy-start) | copy-done | bytes 1572888
  8.2 3.9 %shard_map.122 = (f32[22,96,96]{2,1,0:T(8,128)S(1)}, f32[11,96,96]{2,1,0:T(8,128)}) custom-call(f32[3,32,4096]{2,1,0:T(8,128)S(1)} %bitcast.21, bf16[2,96,384]{2,1,0:T(8,128)(2,1)S(1)} %get-tuple-element.40.wz_ref.refs_9_, bf16[2,96,384]{2,1,0:T(8,128)(2,1)S(1)} %get-tuple-element.39.wy_ref.refs_10_), custom_call_target="tpu_custom_call" | custom-call | flops 4000000000 | bytes 1024 | tf_op jit(solution)/shard_map/pallas_call | solution.py:444
  12.1 1.0 copy-done.9
  13.1 2.9 %collective-permute-start = (f32[11,96,96]{2,1,0:T(8,128)}, f32[11,96,96]{2,1,0:T(8,128)}, u32[]{:S(2)}, u32[]{:S(2)}) collective-permute-start(f32[11,96,96]{2,1,0:T(8,128)} %get-tuple-element.21), channel_id=1, source_target_pairs={{0,2},{2,0},{1,3},{3,1},{4,6},{6,4},{5,7},{7,5},{8,10},{10,8},{9,1... | collective-permute-start | bytes 1216520 | tf_op jit(solution)/shard_map/ppermute | solution.py:490
  16.0 0.0 copy-done.1
  16.0 0.9 constant_dynamic-slice_fusion
  17.0 3.6 %collective-permute-start.4 = (f32[3,16,4096]{2,1,0:T(8,128)}, f32[3,16,4096]{2,1,0:T(8,128)}, u32[]{:S(2)}, u32[]{:S(2)}) collective-permute-start(f32[3,16,4096]{2,1,0:T(8,128)} %constant_dynamic-slice_fusion), channel_id=1, source_target_pairs={{4,0},{8,4},{12,8},{0,12},{5,1},{9,5},{13,9},{1,13},{6,2},{10,6},{... | collective-permute-start | bytes 2359304 | tf_op jit(solution)/shard_map/ppermute | solution.py:488
  20.5 0.0 copy-done.2
  20.6 0.4 collective-permute-start.3
  21.0 6.5 %shard_map.123.g_ref = f32[22,96,96]{2,1,0:T(8,128)S(1)} custom-call(f32[3,32,4096]{2,1,0:T(8,128)S(1)} %bitcast.23, f32[3,32,4096]{2,1,0:T(8,128)S(1)} %bitcast.27, bf16[2,96,384]{2,1,0:T(8,128)(2,1)S(1)} %get-tuple-element.40.wz_ref.refs_9_, bf16[2,96,384]{2,1,0:T(8,128)(2,1)S(1)} %get-tuple-element.39.wy_ref.refs_10_), custom_call_target="tpu_custom_call" | custom-call | flops 14000000000 | bytes 1024 | tf_op jit(solution)/shard_map/pallas_call | solution.py:444
  27.4 0.0 copy-start.7
  27.5 1.0 copy-done.7
  30.7 0.1 fusion.3
  30.8 1.6 %dynamic-slice_bitcast_fusion.3 = bf16[2,2,2,96,96]{4,3,2,1,0:T(8,128)(2,1)} fusion(bf16[4,2,2,2,2,96,96]{6,5,4,3,2,1,0:T(8,128)(2,1)} %constant.63.clone, s32[]{:T(128)S(6)} %select_n.40, s32[]{:T(128)S(6)} %select_n.41), kind=kLoop, calls=%fused_computation.5 | loop fusion | bytes 294920 | tf_op jit(solution)/shard_map/squeeze | solution.py:472
  32.4 0.0 collective-permute-done.refs_1_
  32.4 0.0 collective-permute-start.1
  32.4 3.7 %shard_map.124.f_ref = f32[22,96,96]{2,1,0:T(8,128)S(1)} custom-call(f32[3,32,4096]{2,1,0:T(8,128)S(1)} %bitcast.24, f32[3,32,4096]{2,1,0:T(8,128)S(1)} %bitcast.28, bf16[2,96,384]{2,1,0:T(8,128)(2,1)S(1)} %get-tuple-element.40.wz_ref.refs_9_, bf16[2,96,384]{2,1,0:T(8,128)(2,1)S(1)} %get-tuple-element.39.wy_ref.refs_10_), custom_call_target="tpu_custom_call" | custom-call | flops 1000000000 | bytes 1024 | tf_op jit(solution)/shard_map/pallas_call | solution.py:444
  36.1 0.0 copy-start.3
  36.1 1.0 copy-done.3
  37.1 0.1 broadcast_in_dim.9
  37.2 0.1 broadcast_in_dim_reshape.3.refs_5_
  37.3 1.3 %dynamic-slice_bitcast_fusion.1.refs_11_.xt_ref = bf16[2,2,2,96,384]{4,3,2,1,0:T(8,128)(2,1)S(1)} fusion(bf16[4,2,2,2,2,96,384]{6,5,4,3,2,1,0:T(8,128)(2,1)} %constant.64.clone, s32[]{:T(128)S(6)} %select_n.40, s32[]{:T(128)S(6)} %select_n.41), kind=kLoop, calls=%fused_computation.2 | loop fusion | bytes 1179656 | tf_op jit(solution)/shard_map/squeeze | solution.py:472
  38.6 1.1 reverse_select_fusion.refs_6_
  39.7 0.0 collective-permute-done.1.refs_2_
  39.7 0.0 copy-done.5
  39.7 0.0 copy-done.6
  39.7 0.0 copy-done.10
  39.7 0.0 copy-start.4
  39.7 26.1 %shard_map.125 = (f32[12,48,256]{2,1,0:T(8,128)S(1)}, f32[3072,96]{1,0:T(8,128)S(1)}) custom-call(f32[22,96,96]{2,1,0:T(8,128)S(1)} %copy-done.10, f32[11,96,96]{2,1,0:T(8,128)} %collective-permute-done.refs_1_, f32[11,96,96]{2,1,0:T(8,128)} %collective-permute-done.1.refs_2_, f32[3,32,4096]{2,1,0:T(8,128)} %bitcast.20, f32[3,32,4096]{2,1,0:T(8,128)} %bitcast.25, ...), custom_call_target="tpu_custom_call" | custom-call | flops 24999999488 | bytes 1024 | tf_op jit(solution)/shard_map/pallas_call | solution.py:444
  65.8 0.7 collective-permute-start.2
  66.5 7.8 %shard_map.126.refs_0_ = f32[23,48,256]{2,1,0:T(8,128)S(1)} custom-call(f32[3072,96]{1,0:T(8,128)S(1)} %get-tuple-element.28.coupled_ref, bf16[2,96,384]{2,1,0:T(8,128)(2,1)S(1)} %get-tuple-element.39.wy_ref.refs_10_, bf16[2,2,2,96,384]{4,3,2,1,0:T(8,128)(2,1)S(1)} %dynamic-slice_bitcast_fusion.1.refs_11_.xt_ref, f32[22,96,96]{2,1,0:T(8,128)S(1)} %copy-done.8, ...), custom_call_target="tpu_custom_call" | custom-call | flops 3000000000 | bytes 1024 | tf_op jit(solution)/shard_map/pallas_call | solution.py:444
  74.3 0.0 copy-start.11
  74.4 0.0 collective-permute-done.4
  74.4 0.0 collective-permute-done.3.refs_2_
  74.4 1.5 %collective-permute-start.6 = (f32[23,48,256]{2,1,0:T(8,128)S(1)}, f32[23,48,256]{2,1,0:T(8,128)S(1)}, u32[]{:S(2)}, u32[]{:S(2)}) collective-permute-start(f32[23,48,256]{2,1,0:T(8,128)S(1)} %shard_map.126.refs_0_), channel_id=1, source_target_pairs={{0,2},{2,0},{1,3},{3,1},{4,6},{6,4},{5,7},{7,5},{8,10},{10,8},{9,1... | collective-permute-start | bytes 3391496 | tf_op jit(solution)/shard_map/ppermute | solution.py:515
  75.9 6.2 %collective-permute-done.2 = f32[12,48,256]{2,1,0:T(8,128)S(1)} collective-permute-done((f32[12,48,256]{2,1,0:T(8,128)S(1)}, f32[12,48,256]{2,1,0:T(8,128)S(1)}, u32[]{:S(2)}, u32[]{:S(2)}) %collective-permute-start.2) | collective-permute-done | bytes 589856 | tf_op jit(solution)/shard_map/ppermute | solution.py:515
  82.0 0.1 add.37.refs_0_
  82.1 0.1 collective-permute-start.5
  82.2 1.5 %pad_maximum_fusion.refs_2_ = f32[3,32,4096]{2,1,0:T(8,128)S(1)} fusion(f32[3,16,4096]{2,1,0:T(8,128)} %collective-permute-done.4), kind=kLoop, calls=%fused_computation | loop fusion | flops 393216 | bytes 2359296 | tf_op jit(solution)/shard_map/concatenate | solution.py:528
  83.7 0.5 collective-permute-done.5.refs_1_
  84.2 9.2 %shard_map.127 = f32[3,32,4096]{2,1,0:T(8,128)S(1)} custom-call(f32[12,48,256]{2,1,0:T(8,128)S(1)} %add.37.refs_0_, f32[12,48,256]{2,1,0:T(8,128)S(1)} %collective-permute-done.5.refs_1_, f32[3,32,4096]{2,1,0:T(8,128)S(1)} %pad_maximum_fusion.refs_2_, bf16[2,2,384,96]{3,2,1,0:T(8,128)(2,1)S(1)} %dynamic-slice_bitcast_fusion.2.refs_3_, ...), custom_call_target="tpu_custom_call" | custom-call | flops 100000000 | bytes 1024 | tf_op jit(solution)/shard_map/pallas_call | solution.py:444
  93.4 0.9 dynamic-slice_bitcast_fusion
  94.3 11.5 %collective-permute-done.6.refs_1_ = f32[23,48,256]{2,1,0:T(8,128)S(1)} collective-permute-done((f32[23,48,256]{2,1,0:T(8,128)S(1)}, f32[23,48,256]{2,1,0:T(8,128)S(1)}, u32[]{:S(2)}, u32[]{:S(2)}) %collective-permute-start.6) | collective-permute-done | bytes 1130528 | tf_op jit(solution)/shard_map/ppermute | solution.py:515
  105.9 11.2 %shard_map.128 = f32[3,32,4096]{2,1,0:T(8,128)} custom-call(f32[23,48,256]{2,1,0:T(8,128)S(1)} %shard_map.126.refs_0_, f32[23,48,256]{2,1,0:T(8,128)S(1)} %collective-permute-done.6.refs_1_, f32[3,32,4096]{2,1,0:T(8,128)} %collective-permute-done.3.refs_2_, bf16[2,2,384,96]{3,2,1,0:T(8,128)(2,1)S(1)} %dynamic-slice_bitcast_fusion.2.refs_3_, ...), custom_call_target="tpu_custom_call" | custom-call | flops 10000000000 | bytes 1024 | tf_op jit(solution)/shard_map/pallas_call | solution.py:444
  (11 shorter events, 0.1 us)
Async XLA Ops:
  6.8 1.4 %copy-start = (f32[1,3,32,4096]{3,2,1,0:T(8,128)S(1)}, f32[1,3,32,4096]{3,2,1,0:T(8,128)}, u32[]{:S(2)}) copy-start(f32[1,3,32,4096]{3,2,1,0:T(8,128)} %param.11) | copy-start | bytes 4718596
  8.2 7.8 %copy-start.1 = (f32[1,3,32,4096]{3,2,1,0:T(8,128)S(1)}, f32[1,3,32,4096]{3,2,1,0:T(8,128)}, u32[]{:S(2)}) copy-start(f32[1,3,32,4096]{3,2,1,0:T(8,128)} %param.11) | copy-start | bytes 4718596
  12.1 1.0 copy-start.9
  13.1 7.5 %copy-start.2 = (f32[1,1,3,32,4096]{4,3,2,1,0:T(8,128)S(1)}, f32[1,1,3,32,4096]{4,3,2,1,0:T(8,128)}, u32[]{:S(2)}) copy-start(f32[1,1,3,32,4096]{4,3,2,1,0:T(8,128)} %param.12) | copy-start | bytes 4718596
  13.1 19.3 %collective-permute-start = (f32[11,96,96]{2,1,0:T(8,128)}, f32[11,96,96]{2,1,0:T(8,128)}, u32[]{:S(2)}, u32[]{:S(2)}) collective-permute-start(f32[11,96,96]{2,1,0:T(8,128)} %get-tuple-element.21), channel_id=1, source_target_pairs={{0,2},{2,0},{1,3},{3,1},{4,6},{6,4},{5,7},{7,5},{8,10},{10,8},{9,1... | collective-permute-start | bytes 1216520 | tf_op jit(solution)/shard_map/ppermute | solution.py:490
  17.0 57.4 %collective-permute-start.4 = (f32[3,16,4096]{2,1,0:T(8,128)}, f32[3,16,4096]{2,1,0:T(8,128)}, u32[]{:S(2)}, u32[]{:S(2)}) collective-permute-start(f32[3,16,4096]{2,1,0:T(8,128)} %constant_dynamic-slice_fusion), channel_id=1, source_target_pairs={{4,0},{8,4},{12,8},{0,12},{5,1},{9,5},{13,9},{1,13},{6,2},{10,6},{... | collective-permute-start | bytes 2359304 | tf_op jit(solution)/shard_map/ppermute | solution.py:488
  20.6 53.8 %collective-permute-start.3 = (f32[3,32,4096]{2,1,0:T(8,128)S(1)}, f32[3,32,4096]{2,1,0:T(8,128)}, u32[]{:S(2)}, u32[]{:S(2)}) collective-permute-start(f32[3,32,4096]{2,1,0:T(8,128)S(1)} %bitcast.26), channel_id=1, source_target_pairs={{0,12},{4,0},{8,4},{12,8},{1,5},{5,9},{9,13},{13,1},{2,14},{6,2},{... | collective-permute-start | bytes 4718600 | tf_op jit(solution)/shard_map/ppermute | solution.py:486
  27.4 1.0 copy-start.7
  32.4 7.3 %collective-permute-start.1 = (f32[11,96,96]{2,1,0:T(8,128)}, f32[11,96,96]{2,1,0:T(8,128)}, u32[]{:S(2)}, u32[]{:S(2)}) collective-permute-start(f32[11,96,96]{2,1,0:T(8,128)} %collective-permute-done.refs_1_), channel_id=1, source_target_pairs={{0,1},{1,0},{2,3},{3,2},{4,5},{5,4},{6,7},{7,6},{8,9},{9,8},{10,11... | collective-permute-start | bytes 1216520 | tf_op jit(solution)/shard_map/ppermute | solution.py:491
  36.1 1.0 copy-start.3
  37.1 2.6 %copy-start.5 = (bf16[2,128,288]{2,1,0:T(8,128)(2,1)S(1)}, bf16[2,128,288]{2,1,0:T(8,128)(2,1)}, u32[]{:S(2)}) copy-start(bf16[2,128,288]{2,1,0:T(8,128)(2,1)} %constant.66.clone.refs_7_.refs_4_) | copy-start | bytes 442372
  37.1 2.6 %copy-start.6 = (bf16[2,128,288]{2,1,0:T(8,128)(2,1)S(1)}, bf16[2,128,288]{2,1,0:T(8,128)(2,1)}, u32[]{:S(2)}) copy-start(bf16[2,128,288]{2,1,0:T(8,128)(2,1)} %constant.67.clone.refs_8_.refs_5_) | copy-start | bytes 442372
  37.1 2.6 %copy-start.10 = (f32[22,96,96]{2,1,0:T(8,128)S(1)}, f32[22,96,96]{2,1,0:T(8,128)}, u32[]{:S(2)}) copy-start(f32[22,96,96]{2,1,0:T(8,128)} %copy-done.9) | copy-start | bytes 2433028
  39.7 26.8 %copy-start.4 = (f32[22,96,96]{2,1,0:T(8,128)S(1)}, f32[22,96,96]{2,1,0:T(8,128)}, u32[]{:S(2)}) copy-start(f32[22,96,96]{2,1,0:T(8,128)} %copy-done.3) | copy-start | bytes 2433028
  39.7 26.8 %copy-start.8 = (f32[22,96,96]{2,1,0:T(8,128)S(1)}, f32[22,96,96]{2,1,0:T(8,128)}, u32[]{:S(2)}) copy-start(f32[22,96,96]{2,1,0:T(8,128)} %copy-done.7) | copy-start | bytes 2433028
  65.8 16.2 %collective-permute-start.2 = (f32[12,48,256]{2,1,0:T(8,128)S(1)}, f32[12,48,256]{2,1,0:T(8,128)S(1)}, u32[]{:S(2)}, u32[]{:S(2)}) collective-permute-start(f32[12,48,256]{2,1,0:T(8,128)S(1)} %get-tuple-element.25), channel_id=1, source_target_pairs={{0,2},{2,0},{1,3},{3,1},{4,6},{6,4},{5,7},{7,5},{8,10},{10,8},{9,1... | collective-permute-start | bytes 1769480 | tf_op jit(solution)/shard_map/ppermute | solution.py:515
  74.3 7.8 %copy-start.11 = (bf16[2,2,2,384,96]{4,3,2,1,0:T(8,128)(2,1)S(1)}, bf16[2,2,2,384,96]{4,3,2,1,0:T(8,128)(2,1)}, u32[]{:S(2)}) copy-start(bf16[2,2,2,384,96]{4,3,2,1,0:T(8,128)(2,1)} %constant.65.clone) | copy-start | bytes 1769476
  74.4 31.5 %collective-permute-start.6 = (f32[23,48,256]{2,1,0:T(8,128)S(1)}, f32[23,48,256]{2,1,0:T(8,128)S(1)}, u32[]{:S(2)}, u32[]{:S(2)}) collective-permute-start(f32[23,48,256]{2,1,0:T(8,128)S(1)} %shard_map.126.refs_0_), channel_id=1, source_target_pairs={{0,2},{2,0},{1,3},{3,1},{4,6},{6,4},{5,7},{7,5},{8,10},{10,8},{9,1... | collective-permute-start | bytes 3391496 | tf_op jit(solution)/shard_map/ppermute | solution.py:515
  82.1 2.1 %collective-permute-start.5 = (f32[12,48,256]{2,1,0:T(8,128)S(1)}, f32[12,48,256]{2,1,0:T(8,128)S(1)}, u32[]{:S(2)}, u32[]{:S(2)}) collective-permute-start(f32[12,48,256]{2,1,0:T(8,128)S(1)} %add.37.refs_0_), channel_id=1, source_target_pairs={{0,1},{1,0},{2,3},{3,2},{4,5},{5,4},{6,7},{7,6},{8,9},{9,8},{10,11... | collective-permute-start | bytes 1769480 | tf_op jit(solution)/shard_map/ppermute | solution.py:523
